TPU v7x, 512 devices: a whole 4x8x8 slice. The times are simulated.
512 devices in a mesh: replica: 8 (over z), pipe: 4 (over x), tensor: 16 (over y, core).
Axes of the slice: x: 4, y: 8, z: 8, core: 2. Of those that a mesh axis runs over, the one named last changes fastest.
Arguments:
- queries: bfloat16 [1024, 8192], P('replica', ('pipe', 'tensor')), parts along dimension 0, may hold values from -128 to 128, as said below
- cache_keys: bfloat16 [32, 4096, 1024], P('replica', 'tensor', 'pipe'), parts along dimension 0, may hold values from -4 to 4
- cache_values: bfloat16 [32, 4096, 1024], P('replica', 'tensor', 'pipe'), parts along dimension 0, may hold values from -6 to 6
- prefix_lengths: int32 [32], P('replica'), parts along dimension 0, may hold values from 2048 to 4064
- residual_in: bfloat16 [1024, 8192], P('replica', ('pipe', 'tensor')), parts along dimension 0, may hold values from -64 to 64
- out_weight: bfloat16 [8192, 4, 2048], P('pipe', None, 'tensor'), may hold values from -0.0625 to 0.0625
- norm_gain: float32 [8192], P(('pipe', 'tensor')), may hold values from 0.1 to 1.9
Outputs:
- residual_out: bfloat16 [1024, 8192], P('replica', ('pipe', 'tensor')), parts along dimension 0
- normed: bfloat16 [1024, 8192], P('replica', ('pipe', 'tensor')), parts along dimension 0
There are 8 independent parts, one for each index of `replica`. A program takes and returns all parts, laid end to end along the dimension named above; an argument that names none is the same for every part. Nothing has to cross between parts.
Inputs may be any that keep to these rules, and one draw needn't show every extreme that they name: `queries`: entries of the query rows; some rows may be much longer than others. The span's own keys and values already stand in the cache, in slots prefix_lengths[r] to prefix_lengths[r] + 31; later slots hold unused entries.
All inputs are finite; a program needn't handle non-finite values.
Results may differ from a plain program's by a relative error of at most 0.018.
Values may be sent and summed in bfloat16 or wider, within the bound.
No kernel may reach another device: no remote copies, remote signals or barrier semaphores. Data moves between devices by JAX's collectives and lax.ppermute only.
A program may use at most 64 MiB of HBM per device.

v0:
```python
import math

import jax
import jax.numpy as jnp
from jax import lax
from jax.sharding import PartitionSpec as P

D = 8192
HD = 128


masked_value = -1e30
epsilon = 1e-05


def joined_along(tiles, dim):
    shape = list(tiles.shape[1:])
    shape[dim] *= tiles.shape[0]
    return jnp.moveaxis(tiles, 0, dim).reshape(shape)


def from_everyone(shard, axis):
    copies = jnp.broadcast_to(shard, (lax.axis_size(axis), *shard.shape))
    return lax.all_to_all(copies, axis, split_axis=0, concat_axis=0, tiled=True)


def gathered_copies(shard, axis, dim):
    return joined_along(from_everyone(shard, axis), dim)


def of_everyone(shard, axis):
    return from_everyone(shard, axis).max(axis=0)


def in_blocks(shard, dim, length):
    shape = shard.shape
    tiles = shard.reshape(*shape[:dim], length, shape[dim] // length, *shape[dim + 1 :])
    return jnp.moveaxis(tiles, dim, 0)


def sent_and_summed(shard, axis, dim):
    tiles = in_blocks(shard, dim, lax.axis_size(axis))
    arrived = lax.all_to_all(tiles, axis, split_axis=0, concat_axis=0, tiled=True)
    return arrived.astype(jnp.float32).sum(axis=0)


def side_by_side(arrays, axis, dim, along):
    columns = [a.reshape(*a.shape[:along], -1) for a in arrays]
    both = jnp.concatenate(columns, axis=along)
    out, at, finished = (sent_and_summed(both, axis, dim), 0, [])
    for a, column in zip(arrays, columns):
        slab = out[..., at : at + column.shape[along]]
        finished.append(slab.reshape(*slab.shape[:along], *a.shape[along:]))
        at += column.shape[along]
    return tuple(finished)


def over_copies(shard, axis):
    everything = from_everyone(shard, axis)
    return jnp.sum(everything, axis=0)


def on_device(
    queries, cache_keys, cache_values, prefix_lengths, residual_in, out_weight, norm_gain
):
    tok_rows = queries.shape[0]
    requests = prefix_lengths.shape[0]
    span_len = tok_rows // requests
    slot_count = cache_keys.shape[1]
    local_groups = cache_keys.shape[2] // HD
    gathered = gathered_copies(queries, "tensor", 1)
    heads_here = gathered.shape[1] // HD
    group_size = heads_here // local_groups
    queries_here = gathered.reshape(requests, span_len, local_groups, group_size, HD)
    keys_here = cache_keys.reshape(requests, slot_count, local_groups, HD)
    values_here = cache_values.reshape(requests, slot_count, local_groups, HD)
    scores = jnp.einsum(
        "rcghd,rjgd->rcghj", queries_here, keys_here, preferred_element_type=jnp.float32
    ) * (1.0 / math.sqrt(HD))
    first_slot = lax.axis_index("tensor") * slot_count
    slot_index = first_slot + jnp.arange(slot_count, dtype=jnp.int32)
    limits = prefix_lengths[:, None] + jnp.arange(span_len, dtype=jnp.int32)[None, :]
    visible = (slot_index[None, None, :] <= limits[:, :, None])[:, :, None, None, :]
    masked = jnp.where(visible, scores, masked_value)
    row_peak = jnp.max(masked, axis=-1)
    weights = jnp.where(visible, jnp.exp(masked - row_peak[..., None]), 0.0)
    row_total = jnp.sum(weights, axis=-1)
    weighted = jnp.einsum(
        "rcghj,rjgd->rcghd",
        weights.astype(jnp.bfloat16),
        values_here,
        preferred_element_type=jnp.float32,
    )
    row_peak = row_peak.reshape(tok_rows, heads_here)
    row_total = row_total.reshape(tok_rows, heads_here)
    weighted = weighted.reshape(tok_rows, heads_here, HD)
    overall = of_everyone(row_peak, "tensor")
    factor = jnp.exp(row_peak - overall)
    share_sum, share_total = side_by_side(
        (
            (weighted * factor[..., None]).astype(jnp.bfloat16),
            (row_total * factor).astype(jnp.bfloat16),
        ),
        "tensor",
        1,
        2,
    )
    own_heads = (share_sum / share_total[..., None]).astype(jnp.bfloat16).reshape(tok_rows, -1)
    attended = gathered_copies(own_heads, "tensor", 1)
    col_groups = out_weight.shape[1]
    col_width = out_weight.shape[2]
    partial_value = jnp.dot(
        attended,
        out_weight.reshape(out_weight.shape[0], col_groups * col_width),
        preferred_element_type=jnp.float32,
    )
    projected = sent_and_summed(
        partial_value.reshape(tok_rows, col_groups, col_width).astype(jnp.bfloat16), "pipe", 1
    ).reshape(tok_rows, col_width)
    updated = residual_in.astype(jnp.float32) + projected
    squares = over_copies(jnp.sum(updated * updated, axis=1), ("pipe", "tensor"))
    normed = updated * lax.rsqrt(squares / D + epsilon)[:, None] * norm_gain[None, :]
    return (updated.astype(jnp.bfloat16), normed.astype(jnp.bfloat16))


def solution(mesh):
    in_specs = (
        P("replica", ("pipe", "tensor")),
        P("replica", "tensor", "pipe"),
        P("replica", "tensor", "pipe"),
        P("replica"),
        P("replica", ("pipe", "tensor")),
        P("pipe", None, "tensor"),
        P(("pipe", "tensor")),
    )
    out_specs = (P("replica", ("pipe", "tensor")), P("replica", ("pipe", "tensor")))
    return jax.shard_map(
        on_device, mesh=mesh, in_specs=in_specs, out_specs=out_specs, check_vma=False
    )
```

profile of v0, /device:TPU:1, one launch (start us, length us, event | category | flops | bytes accessed | tf_op | source)
XLA Modules:
  0.0 116.6 jit_solution(15257031075614029294)
XLA Ops:
  0.6 1.7 %broadcast_in_dim.40 = bf16[16,128,128]{2,1,0:T(8,128)(2,1)} broadcast(bf16[128,128]{1,0:T(8,128)(2,1)} %param.7), dimensions={1,2} | broadcast | bytes 557056 | tf_op jit(solution)/shard_map/broadcast_in_dim | solution.py:23
  2.4 10.2 %all-to-all-start = ((bf16[16,128,128]{2,1,0:T(8,128)(2,1)}), bf16[16,128,128]{2,1,0:T(8,128)(2,1)S(1)}, u32[]{:S(2)}, u32[]{:S(2)}) async-start(bf16[16,128,128]{2,1,0:T(8,128)(2,1)} %broadcast_in_dim.40), calls=%async_computation | async-start | bytes 1048576 | tf_op jit(solution)/shard_map/all_to_all | solution.py:24
  12.6 1.2 reshape.117
  14.1 15.8 %all-to-all-done = bf16[16,128,128]{2,1,0:T(8,128)(2,1)S(1)} async-done(((bf16[16,128,128]{2,1,0:T(8,128)(2,1)}), bf16[16,128,128]{2,1,0:T(8,128)(2,1)S(1)}, u32[]{:S(2)}, u32[]{:S(2)}) %all-to-all-start) | async-done | bytes 524320 | tf_op jit(solution)/shard_map/all_to_all | solution.py:24
  29.9 1.8 %fusion = (f32[4,32,2,8]{1,3,2,0:T(8,128)S(1)}, f32[4,2,256,32,8]{2,3,4,1,0:T(8,128)}) fusion(pred[4,32,256]{2,1,0:T(8,128)(4,1)S(1)} %broadcast_compare_fusion, bf16[4,32,2,8,128]{4,1,0,3,2:T(8,128)(2,1)S(1)} %bitcast.63, bf16[4,256,2,128,1]{3,2,1,0,4:T(2,128)(2,1)S(1)} %bitcast.64), kind=kOutput, calls=%fused_computation.3 | convolution fusion | flops 135788544 | bytes 3186688 | tf_op jit(solution)/shard_map/rcghd,rjgd->rcghj/dot_general | solution.py:77
  31.9 2.4 %fusion.2 = (bf16[4,32,2,8,256]{4,1,3,2,0:T(8,128)(2,1)S(1)}, f32[4,32,2,8]{1,3,2,0:T(8,128)S(1)}) fusion(f32[4,2,256,32,8]{2,3,4,1,0:T(8,128)} %get-tuple-element.7, f32[4,32,2,8]{1,3,2,0:T(8,128)S(1)} %get-tuple-element.6, pred[4,32,256]{2,1,0:T(8,128)(4,1)S(1)} %broadcast_compare_fusion), kind=kLoop, calls=%fused_computation.5 | loop fusion | flops 3143680 | bytes 3194880 | tf_op jit(solution)/shard_map/convert_element_type | solution.py:90
  34.3 0.6 broadcast_in_dim.43
  35.0 3.4 %all-to-all-start.1 = ((f32[16,128,16]{1,2,0:T(8,128)}), f32[16,128,16]{1,2,0:T(8,128)S(1)}, u32[]{:S(2)}, u32[]{:S(2)}) async-start(f32[16,128,16]{1,2,0:T(8,128)} %broadcast_in_dim.43), calls=%async_computation.1 | async-start | bytes 262144 | tf_op jit(solution)/shard_map/all_to_all | solution.py:24
  38.4 0.7 convolution_bitcast_fusion
  39.3 7.5 %all-to-all-done.1 = f32[16,128,16]{1,2,0:T(8,128)S(1)} async-done(((f32[16,128,16]{1,2,0:T(8,128)}), f32[16,128,16]{1,2,0:T(8,128)S(1)}, u32[]{:S(2)}, u32[]{:S(2)}) %all-to-all-start.1) | async-done | bytes 131104 | tf_op jit(solution)/shard_map/all_to_all | solution.py:24
  47.0 0.5 copy.110
  47.4 0.3 multiply_convert_fusion
  48.0 1.0 copy.111
  49.0 21.1 %all_to_all.31 = bf16[16,128,1,129]{1,3,2,0:T(8,128)(2,1)S(1)} all-to-all(bf16[16,128,1,129]{1,3,2,0:T(8,128)(2,1)S(1)} %copy.111), channel_id=1, replica_groups=mesh['replica'=8,'pipe'=4,'tensor'=16] {'tensor'}, dimensions={0} | all-to-all | bytes 1056768 | tf_op jit(solution)/shard_map/all_to_all | solution.py:43
  70.6 0.9 broadcast_in_dim.44
  71.5 3.8 %all-to-all-start.3 = ((bf16[16,128,128]{2,1,0:T(8,128)(2,1)}), bf16[16,128,128]{2,1,0:T(8,128)(2,1)S(1)}, u32[]{:S(2)}, u32[]{:S(2)}) async-start(bf16[16,128,128]{2,1,0:T(8,128)(2,1)} %broadcast_in_dim.44), calls=%async_computation.3 | async-start | bytes 1048576 | tf_op jit(solution)/shard_map/all_to_all | solution.py:24
  75.3 1.7 %copy.141 = bf16[256,8,4,128]{3,1,2,0:T(8,128)(2,1)} copy(bf16[256,8,4,128]{3,2,1,0:T(4,128)(2,1)S(1)} %bitcast.61) | data formatting | bytes 4194304
  77.0 2.9 %copy.115 = bf16[512,2048]{1,0:T(8,128)(2,1)S(1)} copy(bf16[512,2048]{0,1:T(8,128)(2,1)} %bitcast.58) | data formatting | bytes 4194304 | tf_op jit(solution)/shard_map/dot_general | solution.py:112
  79.9 12.7 %all-to-all-done.3 = bf16[16,128,128]{2,1,0:T(8,128)(2,1)S(1)} async-done(((bf16[16,128,128]{2,1,0:T(8,128)(2,1)}), bf16[16,128,128]{2,1,0:T(8,128)(2,1)S(1)}, u32[]{:S(2)}, u32[]{:S(2)}) %all-to-all-start.3) | async-done | bytes 524320 | tf_op jit(solution)/shard_map/all_to_all | solution.py:24
  92.6 0.3 copy.114
  93.2 0.8 fusion.3
  94.1 7.2 %all_to_all.32 = bf16[4,128,1,128]{3,1,2,0:T(8,128)(2,1)S(1)} all-to-all(bf16[4,128,1,128]{3,1,2,0:T(8,128)(2,1)S(1)} %fusion.3), channel_id=1, replica_groups=mesh['replica'=8,'pipe'=4,'tensor'=16] {'pipe'}, dimensions={0} | all-to-all | bytes 262144 | tf_op jit(solution)/shard_map/all_to_all | solution.py:43
  101.5 14.3 %all_to_all.33 = f32[64,1,128]{2,1,0:T(1,128)S(1)} all-to-all(f32[64,1,128]{2,1,0:T(1,128)S(1)} %broadcast_in_dim.45), channel_id=1, replica_groups=mesh['replica'=8,'pipe'=4,'tensor'=16] {'pipe','tensor'}, dimensions={0} | all-to-all | bytes 65536 | tf_op jit(solution)/shard_map/all_to_all | solution.py:24
  115.8 0.7 multiply_convert_fusion.1
  (35 shorter events, 1.9 us)
Async XLA Ops:
  0.6 13.1 %copy-start.1 = (bf16[4,256,256]{2,1,0:T(8,128)(2,1)S(1)}, bf16[4,256,256]{2,1,0:T(8,128)(2,1)}, u32[]{:S(2)}) copy-start(bf16[4,256,256]{2,1,0:T(8,128)(2,1)} %param.9) | copy-start | bytes 1572868
  0.6 13.3 %copy-start.4 = (s32[4]{0:T(128)S(1)}, s32[4]{0:T(128)}, u32[]{:S(2)}) copy-start(s32[4]{0:T(128)} %param.10) | copy-start | bytes 52
  2.4 27.6 %all-to-all-start = ((bf16[16,128,128]{2,1,0:T(8,128)(2,1)}), bf16[16,128,128]{2,1,0:T(8,128)(2,1)S(1)}, u32[]{:S(2)}, u32[]{:S(2)}) async-start(bf16[16,128,128]{2,1,0:T(8,128)(2,1)} %broadcast_in_dim.40), calls=%async_computation | async-start | bytes 1048576 | tf_op jit(solution)/shard_map/all_to_all | solution.py:24
  35.0 11.8 %all-to-all-start.1 = ((f32[16,128,16]{1,2,0:T(8,128)}), f32[16,128,16]{1,2,0:T(8,128)S(1)}, u32[]{:S(2)}, u32[]{:S(2)}) async-start(f32[16,128,16]{1,2,0:T(8,128)} %broadcast_in_dim.43), calls=%async_computation.1 | async-start | bytes 262144 | tf_op jit(solution)/shard_map/all_to_all | solution.py:24
  70.1 5.2 %copy-start = (bf16[2048,4,128]{2,1,0:T(4,128)(2,1)S(1)}, bf16[2048,4,128]{2,1,0:T(4,128)(2,1)}, u32[]{:S(2)}) copy-start(bf16[2048,4,128]{2,1,0:T(4,128)(2,1)} %param.12) | copy-start | bytes 6291460
  71.5 21.1 %all-to-all-start.3 = ((bf16[16,128,128]{2,1,0:T(8,128)(2,1)}), bf16[16,128,128]{2,1,0:T(8,128)(2,1)S(1)}, u32[]{:S(2)}, u32[]{:S(2)}) async-start(bf16[16,128,128]{2,1,0:T(8,128)(2,1)} %broadcast_in_dim.44), calls=%async_computation.3 | async-start | bytes 1048576 | tf_op jit(solution)/shard_map/all_to_all | solution.py:24
  93.0 8.3 %copy-start.2 = (bf16[128,128]{1,0:T(8,128)(2,1)S(1)}, bf16[128,128]{1,0:T(8,128)(2,1)}, u32[]{:S(2)}) copy-start(bf16[128,128]{1,0:T(8,128)(2,1)} %param.11) | copy-start | bytes 98308
  93.0 22.9 %copy-start.3 = (f32[128]{0:T(128)S(1)}, f32[128]{0:T(128)}, u32[]{:S(2)}) copy-start(f32[128]{0:T(128)} %param.13) | copy-start | bytes 1540
where the time goes:
time: 117 us
  blocking collectives  42.6 us (36%)
  waiting for transfers between devices  36 us (31%)
  starting transfers between devices  17.4 us (15%)
  local copies, waits for them, and re-layouts  11.9 us (10%)
  other arithmetic  4.33 us (4%)
  matrix products  3.36 us (3%)
    all_to_all x3, waiting for transfers between devices, from_everyone(): return lax.all_to_all(copies, axis, split_axis=0, concat_axis=0, tiled=True)  36 us
    all_to_all x2, blocking collectives, sent_and_summed(): lax.all_to_all(tiles, axis, split_axis=0, concat_axis=0, tiled=True)  28.3 us
    all_to_all x3, starting transfers between devices, from_everyone(): return lax.all_to_all(copies, axis, split_axis=0, concat_axis=0, tiled=True)  17.4 us
    all_to_all x1, blocking collectives, from_everyone(): return lax.all_to_all(copies, axis, split_axis=0, concat_axis=0, tiled=True)  14.3 us
    broadcast_in_dim x4, local copies, waits for them, and re-layouts, from_everyone(): copies = jnp.broadcast_to(shard, (lax.axis_size(axis), *shard.shape))  3.28 us
    dot_general x1, local copies, waits for them, and re-layouts, on_device(): jnp.dot(attended, out_weight.reshape(out_weight.shape[0], col_groups * co...  2.93 us
    convert_element_type x1, other arithmetic, on_device(): weights.astype(jnp.bfloat16)  2.41 us
  transfers between devices with their start and end apart: 3, of which 3 were waited for; matrix products, arithmetic and copies ran while one was open for 6% of the time, Pallas kernels for 0%

commit v1 on v0

v1 whole, which is shorter than its diff:
```python
import math

import jax
import jax.numpy as jnp
from jax import lax
from jax.experimental import pallas as pl
from jax.experimental.pallas import tpu as pltpu
from jax.sharding import Mesh
from jax.sharding import PartitionSpec as P

HD = 128
SPAN = 32
MASKED = -1e30
FLOOR = -1e29
EPSILON = 1e-05
STATS = 16

VMEM = pl.BlockSpec(memory_space=pltpu.VMEM)
SMEM = pl.BlockSpec(memory_space=pltpu.SMEM)
F32 = jnp.float32
BF16 = jnp.bfloat16


def call(kernel, out_shape, args, in_specs=None, scratch=(), flops=0, moved=0, name=None):
    return pl.pallas_call(
        kernel,
        out_shape=out_shape,
        in_specs=in_specs or [VMEM] * len(args),
        out_specs=jax.tree.map(lambda _: VMEM, out_shape),
        scratch_shapes=list(scratch),
        compiler_params=pltpu.CompilerParams(vmem_limit_bytes=24 * 2**20),
        cost_estimate=pl.CostEstimate(flops=flops, bytes_accessed=moved, transcendentals=0),
        name=name,
    )(*args)


def attend_kernel(place, prefix, queries, keys, values, others, out):
    core = place[0]
    starts = (place[1], place[2])
    slots = keys.shape[1]
    rows = 8 * SPAN
    ahead = lax.broadcasted_iota(jnp.int32, (slots, rows), 0) - lax.rem(
        lax.broadcasted_iota(jnp.int32, (slots, rows), 1), SPAN
    )
    line = lax.broadcasted_iota(jnp.int32, (STATS, rows), 0)
    scale = math.log2(math.e) / math.sqrt(HD)
    for at in range(2):
        request = 2 * core + at
        for group in range(2):
            columns = pl.ds(group * HD, HD)
            wanted = queries[pl.ds(8 * group, 8), pl.ds(SPAN * at, SPAN), :].reshape(rows, HD)
            pieces = (
                (keys[request, :, columns], values[request, :, columns]),
                (others[0, at, :, columns], others[1, at, :, columns]),
            )
            scores = []
            for (key, _), start in zip(pieces, starts):
                score = lax.dot_general(
                    key, wanted, (((1,), (1,)), ((), ())), preferred_element_type=F32
                )
                scores.append(
                    jnp.where(ahead <= prefix[request] - start, score * scale, MASKED)
                )
            peak = jnp.maximum(*[jnp.max(s, axis=0, keepdims=True) for s in scores])
            peak = jnp.maximum(peak, FLOOR).astype(BF16).astype(F32)
            weights = [jnp.exp2(s - peak) for s in scores]
            total = sum(jnp.sum(w, axis=0, keepdims=True) for w in weights)
            summed = sum(
                lax.dot_general(
                    value, w.astype(BF16), (((0,), (0,)), ((), ())), preferred_element_type=F32
                )
                for (_, value), w in zip(pieces, weights)
            )
            scaled = (summed * jnp.where(total > 0, 1.0 / total, 0.0)).astype(BF16)
            high = total.astype(BF16).astype(F32)
            stats = jnp.where(
                line == 0, peak, jnp.where(line == 1, high, jnp.where(line == 2, total - high, 0.0))
            ).astype(BF16)
            for half in range(2):
                to = 4 * at + 2 * group + half
                lanes = slice(half * HD, (half + 1) * HD)
                out[to, pl.ds(0, HD), :] = scaled[:, lanes]
                out[to, pl.ds(HD, STATS), :] = stats[:, lanes]


def combine_kernel(parts, out):
    count = parts.shape[0]
    stats = [parts[i, pl.ds(HD, STATS), :].astype(F32) for i in range(count)]
    peaks = [s[0:1] for s in stats]
    overall = peaks[0]
    for peak in peaks[1:]:
        overall = jnp.maximum(overall, peak)
    shares = [(s[1:2] + s[2:3]) * jnp.exp2(p - overall) for s, p in zip(stats, peaks)]
    inverse = 1.0 / sum(shares)
    summed = jnp.zeros((HD, HD), F32)
    for i in range(count):
        summed += parts[i, pl.ds(0, HD), :].astype(F32) * (shares[i] * inverse)
    attended = summed.T.astype(BF16)
    for i in range(count):
        out[i] = attended


def project_kernel(attended, weight, out, joined):
    for core in range(2):
        for at in range(2):
            for quad in range(4):
                for j in range(4):
                    joined[
                        pl.ds(64 * core + SPAN * at, SPAN), pl.ds((4 * quad + j) * HD, HD)
                    ] = attended[core, 4 * at + quad, pl.ds(SPAN * j, SPAN), :]
    for pair in range(2):
        product = jnp.dot(
            joined[...], weight[:, pl.ds(2 * HD * pair, 2 * HD)], preferred_element_type=F32
        ).astype(BF16)
        out[2 * pair] = product[:, :HD]
        out[2 * pair + 1] = product[:, HD:]


def update_kernel(shares, residual, updated, rounded, squares):
    total = residual[...].astype(F32)
    for i in range(shares.shape[0]):
        total += shares[i].astype(F32)
    updated[...] = total
    rounded[...] = total.astype(BF16)
    own = jnp.sum(total * total, axis=1, keepdims=True)
    row = jnp.broadcast_to(own, total.shape).T[0:8]
    for i in range(squares.shape[0] // 8):
        squares[pl.ds(8 * i, 8), :] = row


def norm_kernel(width, updated, squares, gain, out):
    total = jnp.sum(squares[...], axis=0, keepdims=True)
    factor = lax.rsqrt(total / width + EPSILON)
    column = jnp.broadcast_to(factor, updated.shape).T
    out[...] = (updated[...] * column * gain[...]).astype(BF16)


def on_device(queries, cache_keys, cache_values, prefix_lengths, residual_in, out_weight, norm_gain):
    chips = lax.axis_size("y")
    pipes = lax.axis_size("pipe")
    devices = 2 * chips * pipes
    tokens = queries.shape[0]
    slots = cache_keys.shape[1]
    core = lax.axis_index("core")
    chip = lax.axis_index("y")
    place = jnp.stack([core, (2 * chip + core) * slots, (2 * chip + 1 - core) * slots]).astype(jnp.int32)

    halves = jnp.broadcast_to(queries.reshape(1, 2, tokens // 2, HD), (chips, 2, tokens // 2, HD))
    gathered = lax.all_to_all(
        halves.reshape(2 * chips, tokens // 2, HD), ("y", "core"), 0, 0, tiled=True
    )
    away = jnp.stack(
        [lax.dynamic_slice_in_dim(a, 2 * (1 - core), 2, axis=0) for a in (cache_keys, cache_values)]
    )
    others = lax.ppermute(away, "core", [(0, 1), (1, 0)])

    parts = call(
        attend_kernel,
        jax.ShapeDtypeStruct((chips, HD + STATS, HD), BF16),
        (place, prefix_lengths, gathered, cache_keys, cache_values, others),
        in_specs=[SMEM, SMEM, VMEM, VMEM, VMEM, VMEM],
        flops=4 * 2 * 2 * 512 * 256 * HD,
        moved=2**21,
        name="attend",
    )
    parts = lax.all_to_all(parts, "y", 0, 0, tiled=True)
    own = call(
        combine_kernel,
        jax.ShapeDtypeStruct((chips, HD, HD), BF16),
        (parts,),
        flops=2 * 8 * HD * HD,
        moved=2**19,
        name="combine",
    )
    half = lax.all_to_all(own, "y", 0, 0, tiled=True)
    attended = lax.all_gather(half, "core")

    depth, groups, width = out_weight.shape
    shares = call(
        project_kernel,
        jax.ShapeDtypeStruct((groups, tokens, width), BF16),
        (attended, out_weight.reshape(depth, groups * width)),
        scratch=[pltpu.VMEM((tokens, depth), BF16)],
        flops=2 * tokens * depth * groups * width,
        moved=3 * 2**20,
        name="project",
    )
    shares = lax.all_to_all(shares, "pipe", 0, 0, tiled=True)
    updated, rounded, squares = call(
        update_kernel,
        (
            jax.ShapeDtypeStruct((tokens, width), F32),
            jax.ShapeDtypeStruct((tokens, width), BF16),
            jax.ShapeDtypeStruct((devices, tokens), F32),
        ),
        (shares, residual_in),
        flops=8 * tokens * width,
        moved=2**18,
        name="update",
    )
    squares = lax.all_to_all(
        squares.reshape(devices, 1, tokens), ("pipe", "y", "core"), 0, 0, tiled=True
    ).reshape(devices, tokens)

    normed = call(
        lambda *refs: norm_kernel(devices * width, *refs),
        jax.ShapeDtypeStruct((tokens, width), BF16),
        (updated, squares, norm_gain.reshape(1, width)),
        flops=4 * tokens * width,
        moved=2**18,
        name="norm",
    )
    return rounded, normed


def solution(mesh):
    replica, pipe, tensor = mesh.devices.shape
    mesh = Mesh(
        mesh.devices.reshape(replica, pipe, tensor // 2, 2), ("replica", "pipe", "y", "core")
    )
    features = ("pipe", "y", "core")
    tensor = ("y", "core")
    in_specs = (
        P("replica", features),
        P("replica", tensor, "pipe"),
        P("replica", tensor, "pipe"),
        P("replica"),
        P("replica", features),
        P("pipe", None, tensor),
        P(features),
    )
    out_specs = (P("replica", features), P("replica", features))
    return jax.shard_map(
        on_device, mesh=mesh, in_specs=in_specs, out_specs=out_specs, check_vma=False
    )
```

time: 117 us -> 86.5 us (0.74)
  waiting for transfers between devices: 36 us -> 20.2 us
  local copies, waits for them, and re-layouts: 11.9 us -> 3.89 us
  Pallas kernels: 0 us -> 4.9 us
  other arithmetic: 4.33 us -> 0.13 us
  matrix products: 3.36 us -> 0 us
  blocking collectives: 42.6 us -> 40.5 us
  starting transfers between devices: 17.4 us -> 15.6 us
    all_to_all x3 -> x2, waiting for transfers between devices: 36 us -> 20.2 us  [the longest x1 11.7 us: on_device(): lax.all_to_all(halves.reshape(2 * chips, tokens // 2, HD), ('y', 'core'),...]
    all_to_all x3 -> x2, starting transfers between devices: 17.4 us -> 6.84 us  [the longest x1 3.43 us: on_device(): lax.all_to_all(halves.reshape(2 * chips, tokens // 2, HD), ('y', 'core'),...]
    ppermute x0 -> x1, starting transfers between devices: none -> 8.79 us  [on_device(): others = lax.ppermute(away, 'core', [(0, 1), (1, 0)])]
    all_to_all x3, blocking collectives: 42.6 us -> 36.5 us  [the longest x1 15.1 us: on_device(): parts = lax.all_to_all(parts, 'y', 0, 0, tiled=True)]
    pallas_call x0 -> x5, Pallas kernels: none -> 4.9 us  [call(): pl.pallas_call(kernel, out_shape=out_shape, in_specs=in_specs or [VMEM] *...]
    all_gather x0 -> x1, blocking collectives: none -> 4 us  [on_device(): attended = lax.all_gather(half, 'core')]
    convert_element_type x4 -> x0, other arithmetic: 3.46 us -> none  [the longest x1 2.41 us: on_device(): weights.astype(jnp.bfloat16)]
    dot_general x3 -> x0, matrix products: 3.36 us -> none  [the longest x1 1.81 us: on_device(): jnp.einsum('rcghd,rjgd->rcghj', queries_here, keys_here, preferred_elemen...]
  transfers between devices with their start and end apart: 3 -> 3, of which waited for: 3 -> 2; matrix products, arithmetic and copies ran while one was open for 6% -> 3% of each run, Pallas kernels for 0% -> 0%
where the time goes in v1:
time: 86.5 us; the launch traced here: 86 us
  blocking collectives  40.5 us (47%)
  waiting for transfers between devices  20.2 us (23%)
  starting transfers between devices  15.6 us (18%)
  Pallas kernels  4.9 us (6%)
  local copies, waits for them, and re-layouts  3.89 us (4%)
    all_to_all x1, blocking collectives, on_device(): parts = lax.all_to_all(parts, 'y', 0, 0, tiled=True)  15.1 us
    all_to_all x1, blocking collectives, on_device(): lax.all_to_all(squares.reshape(devices, 1, tokens), ('pipe', 'y', 'core')...  14.2 us
    all_to_all x1, waiting for transfers between devices, on_device(): lax.all_to_all(halves.reshape(2 * chips, tokens // 2, HD), ('y', 'core'),...  11.7 us
    ppermute x1, starting transfers between devices, on_device(): others = lax.ppermute(away, 'core', [(0, 1), (1, 0)])  8.79 us
    all_to_all x1, waiting for transfers between devices, on_device(): half = lax.all_to_all(own, 'y', 0, 0, tiled=True)  8.55 us
    all_to_all x1, blocking collectives, on_device(): shares = lax.all_to_all(shares, 'pipe', 0, 0, tiled=True)  7.22 us
    pallas_call x5, Pallas kernels, call(): pl.pallas_call(kernel, out_shape=out_shape, in_specs=in_specs or [VMEM] *...  4.9 us
    all_gather x1, blocking collectives, on_device(): attended = lax.all_gather(half, 'core')  4 us
  transfers between devices with their start and end apart: 3, of which 2 were waited for; matrix products, arithmetic and copies ran while one was open for 3% of the time, Pallas kernels for 0%

profile of v1, /device:TPU:1, one launch (start us, length us, event | category | flops | bytes accessed | tf_op | source)
XLA Modules:
  0.0 86.0 jit_solution(12348402966284633824)
XLA Ops:
  0.6 0.0 copy-start.1
  0.7 1.1 %dynamic-slice_bitcast_fusion = (bf16[1,2,256,256]{3,2,1,0:T(8,128)(2,1)S(1)}, bf16[1,2,256,256]{3,2,1,0:T(8,128)(2,1)S(1)}) fusion(bf16[4,256,256]{2,1,0:T(8,128)(2,1)} %values.1, s32[]{:T(128)S(6)} %select_n.4, bf16[4,256,256]{2,1,0:T(8,128)(2,1)} %keys.1), kind=kLoop, calls=%fused_computation.2 | loop fusion | bytes 1048580 | tf_op jit(solution)/shard_map/stack | solution.py:152
  1.8 0.1 pad_maximum_fusion
  1.9 8.8 %collective-permute-start = (bf16[2,2,256,256]{3,2,1,0:T(8,128)(2,1)S(1)}, bf16[2,2,256,256]{3,2,1,0:T(8,128)(2,1)S(1)}, u32[]{:S(2)}, u32[]{:S(2)}) collective-permute-start(bf16[2,2,256,256]{3,2,1,0:T(8,128)(2,1)S(1)} %pad_maximum_fusion), channel_id=1, source_target_pairs={{0,1},{1,0},{2,3},{3,2},{4,5},{5,4},{6,7},{7,6},{8,9},{9,8},{10,11... | collective-permute-start | bytes 1572872 | tf_op jit(solution)/shard_map/ppermute | solution.py:155
  10.7 0.8 broadcast_in_dim.8
  11.4 3.4 %all-to-all-start = ((bf16[16,64,128]{2,1,0:T(8,128)(2,1)}), bf16[16,64,128]{2,1,0:T(8,128)(2,1)S(1)}, u32[]{:S(2)}, u32[]{:S(2)}) async-start(bf16[16,64,128]{2,1,0:T(8,128)(2,1)} %bitcast.4), calls=%async_computation | async-start | bytes 524288 | tf_op jit(solution)/shard_map/all_to_all | solution.py:149
  14.9 0.1 pad_add_fusion.place
  15.0 11.7 %all-to-all-done.queries = bf16[16,64,128]{2,1,0:T(8,128)(2,1)S(1)} async-done(((bf16[16,64,128]{2,1,0:T(8,128)(2,1)}), bf16[16,64,128]{2,1,0:T(8,128)(2,1)S(1)}, u32[]{:S(2)}, u32[]{:S(2)}) %all-to-all-start) | async-done | bytes 262176 | tf_op jit(solution)/shard_map/all_to_all | solution.py:149
  26.6 0.0 collective-permute-done.others
  26.7 2.2 %attend.1 = bf16[8,144,128]{2,1,0:T(8,128)(2,1)S(1)} custom-call(s32[3]{0:T(128)S(1)} %pad_add_fusion.place, s32[4]{0:T(128)S(1)} %copy-done.4, bf16[16,64,128]{2,1,0:T(8,128)(2,1)S(1)} %all-to-all-done.queries, bf16[4,256,256]{2,1,0:T(8,128)(2,1)S(1)} %copy-done, bf16[4,256,256]{2,1,0:T(8,128)(2,1)S(1)} %copy-done.1, ...), custom_call_target="tpu_custom_call" | custom-call | flops 268435456 | bytes 2097152 | tf_op jit(solution)/shard_map/attend/pallas_call | solution.py:25
  28.8 15.1 %all_to_all.25.parts = bf16[8,144,128]{2,1,0:T(8,128)(2,1)S(1)} all-to-all(bf16[8,144,128]{2,1,0:T(8,128)(2,1)S(1)} %attend.1), channel_id=1, replica_groups=mesh['replica'=8,'pipe'=4,'y'=8,'core'=2] {'y'}, dimensions={0} | all-to-all | bytes 589824 | tf_op jit(solution)/shard_map/all_to_all | solution.py:166
  43.9 0.9 %combine.1 = bf16[8,128,128]{2,1,0:T(8,128)(2,1)} custom-call(bf16[8,144,128]{2,1,0:T(8,128)(2,1)S(1)} %all_to_all.25.parts), custom_call_target="tpu_custom_call" | custom-call | flops 262144 | bytes 524288 | tf_op jit(solution)/shard_map/combine/pallas_call | solution.py:25
  44.8 3.4 %all-to-all-start.2 = ((bf16[8,128,128]{2,1,0:T(8,128)(2,1)}), bf16[8,128,128]{2,1,0:T(8,128)(2,1)S(1)}, u32[]{:S(2)}, u32[]{:S(2)}) async-start(bf16[8,128,128]{2,1,0:T(8,128)(2,1)} %combine.1), calls=%async_computation.2 | async-start | bytes 524288 | tf_op jit(solution)/shard_map/all_to_all | solution.py:175
  48.2 2.0 %copy.12 = bf16[256,8,4,128]{3,1,2,0:T(8,128)(2,1)S(1)} copy(bf16[256,8,4,128]{3,2,1,0:T(4,128)(2,1)} %bitcast.24) | data formatting | bytes 4194304
  50.1 0.0 copy-start.2
  50.2 0.0 copy-start.3
  50.2 8.6 %all-to-all-done.2 = bf16[8,128,128]{2,1,0:T(8,128)(2,1)S(1)} async-done(((bf16[8,128,128]{2,1,0:T(8,128)(2,1)}), bf16[8,128,128]{2,1,0:T(8,128)(2,1)S(1)}, u32[]{:S(2)}, u32[]{:S(2)}) %all-to-all-start.2) | async-done | bytes 262176 | tf_op jit(solution)/shard_map/all_to_all | solution.py:175
  58.7 4.0 %all-gather = bf16[16,128,128]{2,1,0:T(8,128)(2,1)S(1)} all-gather(bf16[8,128,128]{2,1,0:T(8,128)(2,1)S(1)} %all-to-all-done.2), channel_id=2, replica_groups=mesh['replica'=8,'pipe'=4,'y'=8,'core'=2] {'core'}, dimensions={0}, use_global_device_ids=true | all-gather | bytes 786432 | tf_op jit(solution)/shard_map/all_gather | solution.py:176
  62.7 0.5 project.1
  63.2 7.2 %all_to_all.26.shares = bf16[4,128,128]{2,1,0:T(8,128)(2,1)S(1)} all-to-all(bf16[4,128,128]{2,1,0:T(8,128)(2,1)S(1)} %project.1), channel_id=1, replica_groups=mesh['replica'=8,'pipe'=4,'y'=8,'core'=2] {'pipe'}, dimensions={0} | all-to-all | bytes 262144 | tf_op jit(solution)/shard_map/all_to_all | solution.py:188
  70.4 0.6 update.1
  71.1 14.2 %all_to_all.27 = f32[64,1,128]{2,1,0:T(1,128)S(1)} all-to-all(f32[64,1,128]{2,1,0:T(1,128)S(1)} %bitcast.22), channel_id=1, replica_groups=mesh['replica'=8,'pipe'=4,'y'=8,'core'=2] {'pipe','y','core'}, dimensions={0} | all-to-all | bytes 65536 | tf_op jit(solution)/shard_map/all_to_all | solution.py:201
  85.3 0.0 copy-done.3
  85.3 0.7 norm.1
  (8 shorter events, 0.0 us)
Async XLA Ops:
  0.6 26.0 %copy-start.1 = (bf16[4,256,256]{2,1,0:T(8,128)(2,1)S(1)}, bf16[4,256,256]{2,1,0:T(8,128)(2,1)}, u32[]{:S(2)}) copy-start(bf16[4,256,256]{2,1,0:T(8,128)(2,1)} %values.1) | copy-start | bytes 1572868
  0.6 26.0 %copy-start = (bf16[4,256,256]{2,1,0:T(8,128)(2,1)S(1)}, bf16[4,256,256]{2,1,0:T(8,128)(2,1)}, u32[]{:S(2)}) copy-start(bf16[4,256,256]{2,1,0:T(8,128)(2,1)} %keys.1) | copy-start | bytes 1572868
  0.7 10.0 %copy-start.5 = (bf16[128,128]{1,0:T(8,128)(2,1)S(1)}, bf16[128,128]{1,0:T(8,128)(2,1)}, u32[]{:S(2)}) copy-start(bf16[128,128]{1,0:T(8,128)(2,1)} %param.7) | copy-start | bytes 98308
  0.7 26.0 %copy-start.4 = (s32[4]{0:T(128)S(1)}, s32[4]{0:T(128)}, u32[]{:S(2)}) copy-start(s32[4]{0:T(128)} %prefix.1) | copy-start | bytes 52
  1.9 24.8 %collective-permute-start = (bf16[2,2,256,256]{3,2,1,0:T(8,128)(2,1)S(1)}, bf16[2,2,256,256]{3,2,1,0:T(8,128)(2,1)S(1)}, u32[]{:S(2)}, u32[]{:S(2)}) collective-permute-start(bf16[2,2,256,256]{3,2,1,0:T(8,128)(2,1)S(1)} %pad_maximum_fusion), channel_id=1, source_target_pairs={{0,1},{1,0},{2,3},{3,2},{4,5},{5,4},{6,7},{7,6},{8,9},{9,8},{10,11... | collective-permute-start | bytes 1572872 | tf_op jit(solution)/shard_map/ppermute | solution.py:155
  11.4 15.2 %all-to-all-start = ((bf16[16,64,128]{2,1,0:T(8,128)(2,1)}), bf16[16,64,128]{2,1,0:T(8,128)(2,1)S(1)}, u32[]{:S(2)}, u32[]{:S(2)}) async-start(bf16[16,64,128]{2,1,0:T(8,128)(2,1)} %bitcast.4), calls=%async_computation | async-start | bytes 524288 | tf_op jit(solution)/shard_map/all_to_all | solution.py:149
  44.8 14.0 %all-to-all-start.2 = ((bf16[8,128,128]{2,1,0:T(8,128)(2,1)}), bf16[8,128,128]{2,1,0:T(8,128)(2,1)S(1)}, u32[]{:S(2)}, u32[]{:S(2)}) async-start(bf16[8,128,128]{2,1,0:T(8,128)(2,1)} %combine.1), calls=%async_computation.2 | async-start | bytes 524288 | tf_op jit(solution)/shard_map/all_to_all | solution.py:175
  50.1 20.3 %copy-start.2 = (bf16[128,128]{1,0:T(8,128)(2,1)S(1)}, bf16[128,128]{1,0:T(8,128)(2,1)}, u32[]{:S(2)}) copy-start(bf16[128,128]{1,0:T(8,128)(2,1)} %residual.1) | copy-start | bytes 98308
  50.2 35.1 %copy-start.3 = (f32[128]{0:T(128)S(1)}, f32[128]{0:T(128)}, u32[]{:S(2)}) copy-start(f32[128]{0:T(128)} %param.13) | copy-start | bytes 1540

commit v2 on v1

--- a/solution.py
+++ b/solution.py
@@ -34,53 +34,57 @@
     )(*args)
 
 
-def attend_kernel(place, prefix, queries, keys, values, others, out):
-    core = place[0]
-    starts = (place[1], place[2])
-    slots = keys.shape[1]
-    rows = 8 * SPAN
+def arrange_kernel(queries, out):
+    heads = queries.shape[0] // 2
+    rows = heads * SPAN
+    blank = jnp.zeros((rows, HD), BF16)
+    for request in range(out.shape[0]):
+        for group in range(2):
+            for of in range(2):
+                out[request, pl.ds(rows * group, rows), pl.ds(HD * of, HD)] = (
+                    queries[pl.ds(heads * group, heads), pl.ds(SPAN * request, SPAN), :].reshape(rows, HD)
+                    if of == group
+                    else blank
+                )
+
+
+def attend_kernel(place, prefix, queries, keys, values, other_keys, other_values, weight, out):
+    del weight
+    starts = (place[0], place[1])
+    requests, slots, width = keys.shape
+    rows = width
     ahead = lax.broadcasted_iota(jnp.int32, (slots, rows), 0) - lax.rem(
         lax.broadcasted_iota(jnp.int32, (slots, rows), 1), SPAN
     )
     line = lax.broadcasted_iota(jnp.int32, (STATS, rows), 0)
     scale = math.log2(math.e) / math.sqrt(HD)
-    for at in range(2):
-        request = 2 * core + at
+    for request in range(requests):
+        wanted = queries[request]
+        scores = []
+        for key, start in zip((keys, other_keys), starts):
+            score = lax.dot_general(
+                key[request], wanted, (((1,), (1,)), ((), ())), preferred_element_type=F32
+            )
+            scores.append(jnp.where(ahead <= prefix[request] - start, score * scale, MASKED))
+        peak = jnp.maximum(*[jnp.max(s, axis=0, keepdims=True) for s in scores])
+        peak = jnp.maximum(peak, FLOOR).astype(BF16).astype(F32)
+        weights = [jnp.exp2(s - peak) for s in scores]
+        total = sum(jnp.sum(w, axis=0, keepdims=True) for w in weights)
+        summed = sum(
+            lax.dot_general(
+                value[request], w.astype(BF16), (((0,), (0,)), ((), ())), preferred_element_type=F32
+            )
+            for value, w in zip((values, other_values), weights)
+        )
+        inverse = jnp.where(total > 0, 1.0 / total, 0.0)
+        high = total.astype(BF16).astype(F32)
+        stats = jnp.where(
+            line == 0, peak, jnp.where(line == 1, high, jnp.where(line == 2, total - high, 0.0))
+        ).astype(BF16)
         for group in range(2):
-            columns = pl.ds(group * HD, HD)
-            wanted = queries[pl.ds(8 * group, 8), pl.ds(SPAN * at, SPAN), :].reshape(rows, HD)
-            pieces = (
-                (keys[request, :, columns], values[request, :, columns]),
-                (others[0, at, :, columns], others[1, at, :, columns]),
-            )
-            scores = []
-            for (key, _), start in zip(pieces, starts):
-                score = lax.dot_general(
-                    key, wanted, (((1,), (1,)), ((), ())), preferred_element_type=F32
-                )
-                scores.append(
-                    jnp.where(ahead <= prefix[request] - start, score * scale, MASKED)
-                )
-            peak = jnp.maximum(*[jnp.max(s, axis=0, keepdims=True) for s in scores])
-            peak = jnp.maximum(peak, FLOOR).astype(BF16).astype(F32)
-            weights = [jnp.exp2(s - peak) for s in scores]
-            total = sum(jnp.sum(w, axis=0, keepdims=True) for w in weights)
-            summed = sum(
-                lax.dot_general(
-                    value, w.astype(BF16), (((0,), (0,)), ((), ())), preferred_element_type=F32
-                )
-                for (_, value), w in zip(pieces, weights)
-            )
-            scaled = (summed * jnp.where(total > 0, 1.0 / total, 0.0)).astype(BF16)
-            high = total.astype(BF16).astype(F32)
-            stats = jnp.where(
-                line == 0, peak, jnp.where(line == 1, high, jnp.where(line == 2, total - high, 0.0))
-            ).astype(BF16)
-            for half in range(2):
-                to = 4 * at + 2 * group + half
-                lanes = slice(half * HD, (half + 1) * HD)
-                out[to, pl.ds(0, HD), :] = scaled[:, lanes]
-                out[to, pl.ds(HD, STATS), :] = stats[:, lanes]
+            part = slice(group * HD, (group + 1) * HD)
+            out[2 * request + group, pl.ds(0, HD), :] = (summed[part, part] * inverse[:, part]).astype(BF16)
+            out[2 * request + group, pl.ds(HD, STATS), :] = stats[:, part]
 
 
 def combine_kernel(parts, out):
@@ -102,12 +106,12 @@
 
 def project_kernel(attended, weight, out, joined):
     for core in range(2):
-        for at in range(2):
-            for quad in range(4):
-                for j in range(4):
-                    joined[
-                        pl.ds(64 * core + SPAN * at, SPAN), pl.ds((4 * quad + j) * HD, HD)
-                    ] = attended[core, 4 * at + quad, pl.ds(SPAN * j, SPAN), :]
+        for place in range(attended.shape[1]):
+            request, group = place // 2, place % 2
+            for j in range(4):
+                joined[
+                    pl.ds(SPAN * request, SPAN), pl.ds((8 * group + 2 * j + core) * HD, HD)
+                ] = attended[core, place, pl.ds(SPAN * j, SPAN), :]
     for pair in range(2):
         product = jnp.dot(
             joined[...], weight[:, pl.ds(2 * HD * pair, 2 * HD)], preferred_element_type=F32
@@ -141,24 +145,32 @@
     devices = 2 * chips * pipes
     tokens = queries.shape[0]
     slots = cache_keys.shape[1]
+    depth, groups, width = out_weight.shape
+    weight = out_weight.reshape(depth, groups * width)
     core = lax.axis_index("core")
     chip = lax.axis_index("y")
-    place = jnp.stack([core, (2 * chip + core) * slots, (2 * chip + 1 - core) * slots]).astype(jnp.int32)
-
-    halves = jnp.broadcast_to(queries.reshape(1, 2, tokens // 2, HD), (chips, 2, tokens // 2, HD))
+    place = jnp.stack([(2 * chip + core) * slots, (2 * chip + 1 - core) * slots]).astype(jnp.int32)
+
     gathered = lax.all_to_all(
-        halves.reshape(2 * chips, tokens // 2, HD), ("y", "core"), 0, 0, tiled=True
-    )
-    away = jnp.stack(
-        [lax.dynamic_slice_in_dim(a, 2 * (1 - core), 2, axis=0) for a in (cache_keys, cache_values)]
-    )
-    others = lax.ppermute(away, "core", [(0, 1), (1, 0)])
-
+        jnp.broadcast_to(queries, (chips, tokens, HD)), "y", 0, 0, tiled=True
+    )
+    swap = [(0, 1), (1, 0)]
+    other_keys = lax.ppermute(cache_keys, "core", swap)
+    other_values = lax.ppermute(cache_values, "core", swap)
+
+    arranged = call(
+        arrange_kernel,
+        jax.ShapeDtypeStruct((cache_keys.shape[0], 2 * HD, 2 * HD), BF16),
+        (gathered,),
+        flops=2**30,
+        moved=2**19,
+        name="arrange",
+    )
     parts = call(
         attend_kernel,
         jax.ShapeDtypeStruct((chips, HD + STATS, HD), BF16),
-        (place, prefix_lengths, gathered, cache_keys, cache_values, others),
-        in_specs=[SMEM, SMEM, VMEM, VMEM, VMEM, VMEM],
+        (place, prefix_lengths, arranged, cache_keys, cache_values, other_keys, other_values, weight),
+        in_specs=[SMEM, SMEM] + [VMEM] * 5 + [pl.BlockSpec(memory_space=pl.ANY)],
         flops=4 * 2 * 2 * 512 * 256 * HD,
         moved=2**21,
         name="attend",
@@ -175,11 +187,10 @@
     half = lax.all_to_all(own, "y", 0, 0, tiled=True)
     attended = lax.all_gather(half, "core")
 
-    depth, groups, width = out_weight.shape
     shares = call(
         project_kernel,
         jax.ShapeDtypeStruct((groups, tokens, width), BF16),
-        (attended, out_weight.reshape(depth, groups * width)),
+        (attended.reshape(2, chips, HD, HD), weight),
         scratch=[pltpu.VMEM((tokens, depth), BF16)],
         flops=2 * tokens * depth * groups * width,
         moved=3 * 2**20,

time: 86.5 us -> 81.2 us (0.939)
  waiting for transfers between devices: 20.2 us -> 0.84 us
  blocking collectives: 40.5 us -> 56.7 us
  starting transfers between devices: 15.6 us -> 14.1 us
    all_to_all x2 -> x1, waiting for transfers between devices: 20.2 us -> 0.83 us  [on_device(): lax.all_to_all(jnp.broadcast_to(queries, (chips, tokens, HD)), 'y', 0, 0,...]
    all_to_all x0 -> x1, blocking collectives: none -> 11.6 us  [on_device(): half = lax.all_to_all(own, 'y', 0, 0, tiled=True)]
    all_to_all x1, blocking collectives: 15.1 us -> 18.1 us  [on_device(): parts = lax.all_to_all(parts, 'y', 0, 0, tiled=True)]
    ppermute x1 -> x2, starting transfers between devices: 8.79 us -> 6.48 us  [the longest x1 4.56 us: on_device(): other_keys = lax.ppermute(cache_keys, 'core', swap)]
    all_gather x1, blocking collectives: 4 us -> 5.57 us  [on_device(): attended = lax.all_gather(half, 'core')]
    another operation x1 -> x0, local copies, waits for them, and re-layouts: 1.15 us -> none  [on_device(): jnp.stack([lax.dynamic_slice_in_dim(a, 2 * (1 - core), 2, axis=0) for a i...]
    all_to_all x2 -> x1, starting transfers between devices: 6.84 us -> 7.65 us  [on_device(): lax.all_to_all(jnp.broadcast_to(queries, (chips, tokens, HD)), 'y', 0, 0,...]
    pallas_call x5 -> x6, Pallas kernels: 4.9 us -> 4.47 us  [call(): pl.pallas_call(kernel, out_shape=out_shape, in_specs=in_specs or [VMEM] *...]
  transfers between devices with their start and end apart: 3 -> 3, of which waited for: 2 -> 1; matrix products, arithmetic and copies ran while one was open for 3% -> 3% of each run, Pallas kernels for 0% -> 0%
where the time goes in v2:
time: 81.2 us; the launch traced here: 80.6 us
  blocking collectives  56.7 us (70%)
  starting transfers between devices  14.1 us (17%)
  Pallas kernels  4.47 us (6%)
  local copies, waits for them, and re-layouts  3.64 us (4%)
  waiting for transfers between devices  0.84 us (1%)
    all_to_all x1, blocking collectives, on_device(): parts = lax.all_to_all(parts, 'y', 0, 0, tiled=True)  18.1 us
    all_to_all x1, blocking collectives, on_device(): lax.all_to_all(squares.reshape(devices, 1, tokens), ('pipe', 'y', 'core')...  14.2 us
    all_to_all x1, blocking collectives, on_device(): half = lax.all_to_all(own, 'y', 0, 0, tiled=True)  11.6 us
    all_to_all x1, starting transfers between devices, on_device(): lax.all_to_all(jnp.broadcast_to(queries, (chips, tokens, HD)), 'y', 0, 0,...  7.65 us
    all_to_all x1, blocking collectives, on_device(): shares = lax.all_to_all(shares, 'pipe', 0, 0, tiled=True)  7.22 us
    all_gather x1, blocking collectives, on_device(): attended = lax.all_gather(half, 'core')  5.57 us
    ppermute x1, starting transfers between devices, on_device(): other_keys = lax.ppermute(cache_keys, 'core', swap)  4.56 us
    pallas_call x6, Pallas kernels, call(): pl.pallas_call(kernel, out_shape=out_shape, in_specs=in_specs or [VMEM] *...  4.47 us
  transfers between devices with their start and end apart: 3, of which 1 were waited for; matrix products, arithmetic and copies ran while one was open for 3% of the time, Pallas kernels for 0%

profile of v2, /device:TPU:1, one launch (start us, length us, event | category | flops | bytes accessed | tf_op | source)
XLA Modules:
  0.0 80.6 jit_solution(7561214851378041678)
XLA Ops:
  0.6 1.5 %broadcast_in_dim.3 = bf16[8,128,128]{2,1,0:T(8,128)(2,1)} broadcast(bf16[128,128]{1,0:T(8,128)(2,1)} %param.7), dimensions={1,2} | broadcast | bytes 294912 | tf_op jit(solution)/shard_map/broadcast_in_dim | solution.py:155
  2.1 7.7 %all-to-all-start = ((bf16[8,128,128]{2,1,0:T(8,128)(2,1)}), bf16[8,128,128]{2,1,0:T(8,128)(2,1)S(1)}, u32[]{:S(2)}, u32[]{:S(2)}) async-start(bf16[8,128,128]{2,1,0:T(8,128)(2,1)} %broadcast_in_dim.3), calls=%async_computation | async-start | bytes 524288 | tf_op jit(solution)/shard_map/all_to_all | solution.py:154
  9.8 4.6 %collective-permute-start = (bf16[4,256,256]{2,1,0:T(8,128)(2,1)}, bf16[4,256,256]{2,1,0:T(8,128)(2,1)}, u32[]{:S(2)}, u32[]{:S(2)}) collective-permute-start(bf16[4,256,256]{2,1,0:T(8,128)(2,1)} %keys.1), channel_id=1, source_target_pairs={{0,1},{1,0},{2,3},{3,2},{4,5},{5,4},{6,7},{7,6},{8,9},{9,8},{10,11... | collective-permute-start | bytes 1572872 | tf_op jit(solution)/shard_map/ppermute | solution.py:158
  14.3 1.9 %collective-permute-start.1 = (bf16[4,256,256]{2,1,0:T(8,128)(2,1)}, bf16[4,256,256]{2,1,0:T(8,128)(2,1)}, u32[]{:S(2)}, u32[]{:S(2)}) collective-permute-start(bf16[4,256,256]{2,1,0:T(8,128)(2,1)} %values.1), channel_id=1, source_target_pairs={{0,1},{1,0},{2,3},{3,2},{4,5},{5,4},{6,7},{7,6},{8,9},{9,8},{10,11... | collective-permute-start | bytes 1572872 | tf_op jit(solution)/shard_map/ppermute | solution.py:159
  16.3 2.0 %copy.12 = bf16[256,8,4,128]{3,1,2,0:T(8,128)(2,1)S(1)} copy(bf16[256,8,4,128]{3,2,1,0:T(4,128)(2,1)} %bitcast.18) | data formatting | bytes 4194304
  18.2 0.0 copy-start
  18.3 0.0 copy-start.1
  18.3 0.0 copy-start.3
  18.3 0.1 pad_add_fusion.place
  18.4 0.8 %all-to-all-done.queries = bf16[8,128,128]{2,1,0:T(8,128)(2,1)S(1)} async-done(((bf16[8,128,128]{2,1,0:T(8,128)(2,1)}), bf16[8,128,128]{2,1,0:T(8,128)(2,1)S(1)}, u32[]{:S(2)}, u32[]{:S(2)}) %all-to-all-start) | async-done | bytes 262176 | tf_op jit(solution)/shard_map/all_to_all | solution.py:154
  19.2 0.1 arrange.1.queries
  19.3 0.0 collective-permute-done.1.other_values
  19.3 0.2 copy-done.1
  19.5 2.4 %attend.1 = bf16[8,144,128]{2,1,0:T(8,128)(2,1)S(1)} custom-call(s32[2]{0:T(128)S(1)} %pad_add_fusion.place, s32[4]{0:T(128)S(1)} %copy-done.3, bf16[4,256,256]{2,1,0:T(8,128)(2,1)S(1)} %arrange.1.queries, bf16[4,256,256]{2,1,0:T(8,128)(2,1)S(1)} %copy-done, bf16[4,256,256]{2,1,0:T(8,128)(2,1)S(1)} %copy-done.1, ...), custom_call_target="tpu_custom_call" | custom-call | flops 268435456 | bytes 2097152 | tf_op jit(solution)/shard_map/attend/pallas_call | solution.py:25
  21.9 18.1 %all_to_all.25.parts = bf16[8,144,128]{2,1,0:T(8,128)(2,1)S(1)} all-to-all(bf16[8,144,128]{2,1,0:T(8,128)(2,1)S(1)} %attend.1), channel_id=1, replica_groups=mesh['replica'=8,'pipe'=4,'y'=8,'core'=2] {'y'}, dimensions={0} | all-to-all | bytes 589824 | tf_op jit(solution)/shard_map/all_to_all | solution.py:178
  40.0 0.2 combine.1
  40.1 0.0 copy-start.2
  40.1 11.6 %all_to_all.26 = bf16[8,128,128]{2,1,0:T(8,128)(2,1)S(1)} all-to-all(bf16[8,128,128]{2,1,0:T(8,128)(2,1)S(1)} %combine.1), channel_id=1, replica_groups=mesh['replica'=8,'pipe'=4,'y'=8,'core'=2] {'y'}, dimensions={0} | all-to-all | bytes 524288 | tf_op jit(solution)/shard_map/all_to_all | solution.py:187
  51.7 5.6 %all-gather = bf16[16,128,128]{2,1,0:T(8,128)(2,1)S(1)} all-gather(bf16[8,128,128]{2,1,0:T(8,128)(2,1)S(1)} %all_to_all.26), channel_id=2, replica_groups=mesh['replica'=8,'pipe'=4,'y'=8,'core'=2] {'core'}, dimensions={0}, use_global_device_ids=true | all-gather | bytes 786432 | tf_op jit(solution)/shard_map/all_gather | solution.py:188
  57.3 0.5 project.1
  57.8 7.2 %all_to_all.27.shares = bf16[4,128,128]{2,1,0:T(8,128)(2,1)S(1)} all-to-all(bf16[4,128,128]{2,1,0:T(8,128)(2,1)S(1)} %project.1), channel_id=1, replica_groups=mesh['replica'=8,'pipe'=4,'y'=8,'core'=2] {'pipe'}, dimensions={0} | all-to-all | bytes 262144 | tf_op jit(solution)/shard_map/all_to_all | solution.py:199
  65.0 0.6 update.1
  65.7 14.2 %all_to_all.28 = f32[64,1,128]{2,1,0:T(1,128)S(1)} all-to-all(f32[64,1,128]{2,1,0:T(1,128)S(1)} %bitcast.16), channel_id=1, replica_groups=mesh['replica'=8,'pipe'=4,'y'=8,'core'=2] {'pipe','y','core'}, dimensions={0} | all-to-all | bytes 65536 | tf_op jit(solution)/shard_map/all_to_all | solution.py:212
  79.9 0.7 norm.1
  (6 shorter events, 0.0 us)
Async XLA Ops:
  2.1 17.1 %all-to-all-start = ((bf16[8,128,128]{2,1,0:T(8,128)(2,1)}), bf16[8,128,128]{2,1,0:T(8,128)(2,1)S(1)}, u32[]{:S(2)}, u32[]{:S(2)}) async-start(bf16[8,128,128]{2,1,0:T(8,128)(2,1)} %broadcast_in_dim.3), calls=%async_computation | async-start | bytes 524288 | tf_op jit(solution)/shard_map/all_to_all | solution.py:154
  9.8 9.5 %collective-permute-start = (bf16[4,256,256]{2,1,0:T(8,128)(2,1)}, bf16[4,256,256]{2,1,0:T(8,128)(2,1)}, u32[]{:S(2)}, u32[]{:S(2)}) collective-permute-start(bf16[4,256,256]{2,1,0:T(8,128)(2,1)} %keys.1), channel_id=1, source_target_pairs={{0,1},{1,0},{2,3},{3,2},{4,5},{5,4},{6,7},{7,6},{8,9},{9,8},{10,11... | collective-permute-start | bytes 1572872 | tf_op jit(solution)/shard_map/ppermute | solution.py:158
  14.3 4.9 %collective-permute-start.1 = (bf16[4,256,256]{2,1,0:T(8,128)(2,1)}, bf16[4,256,256]{2,1,0:T(8,128)(2,1)}, u32[]{:S(2)}, u32[]{:S(2)}) collective-permute-start(bf16[4,256,256]{2,1,0:T(8,128)(2,1)} %values.1), channel_id=1, source_target_pairs={{0,1},{1,0},{2,3},{3,2},{4,5},{5,4},{6,7},{7,6},{8,9},{9,8},{10,11... | collective-permute-start | bytes 1572872 | tf_op jit(solution)/shard_map/ppermute | solution.py:159
  18.2 1.0 %copy-start = (bf16[4,256,256]{2,1,0:T(8,128)(2,1)S(1)}, bf16[4,256,256]{2,1,0:T(8,128)(2,1)}, u32[]{:S(2)}) copy-start(bf16[4,256,256]{2,1,0:T(8,128)(2,1)} %keys.1) | copy-start | bytes 1572868
  18.3 1.2 %copy-start.1 = (bf16[4,256,256]{2,1,0:T(8,128)(2,1)S(1)}, bf16[4,256,256]{2,1,0:T(8,128)(2,1)}, u32[]{:S(2)}) copy-start(bf16[4,256,256]{2,1,0:T(8,128)(2,1)} %values.1) | copy-start | bytes 1572868
  18.3 1.2 %copy-start.3 = (s32[4]{0:T(128)S(1)}, s32[4]{0:T(128)}, u32[]{:S(2)}) copy-start(s32[4]{0:T(128)} %prefix.1) | copy-start | bytes 52
  40.1 24.9 %copy-start.2 = (bf16[128,128]{1,0:T(8,128)(2,1)S(1)}, bf16[128,128]{1,0:T(8,128)(2,1)}, u32[]{:S(2)}) copy-start(bf16[128,128]{1,0:T(8,128)(2,1)} %residual.1) | copy-start | bytes 98308
  51.7 28.2 %copy-start.4 = (f32[128]{0:T(128)S(1)}, f32[128]{0:T(128)}, u32[]{:S(2)}) copy-start(f32[128]{0:T(128)} %param.13) | copy-start | bytes 1540

commit v3 on v2

--- a/solution.py
+++ b/solution.py
@@ -16,7 +16,6 @@
 STATS = 16
 
 VMEM = pl.BlockSpec(memory_space=pltpu.VMEM)
-SMEM = pl.BlockSpec(memory_space=pltpu.SMEM)
 F32 = jnp.float32
 BF16 = jnp.bfloat16
 
@@ -48,24 +47,25 @@
                 )
 
 
-def attend_kernel(place, prefix, queries, keys, values, other_keys, other_values, weight, out):
-    del weight
-    starts = (place[0], place[1])
+def attend_kernel(prefix, queries, keys, values, other_keys, other_values, out):
     requests, slots, width = keys.shape
     rows = width
-    ahead = lax.broadcasted_iota(jnp.int32, (slots, rows), 0) - lax.rem(
-        lax.broadcasted_iota(jnp.int32, (slots, rows), 1), SPAN
-    )
+    slot = lax.broadcasted_iota(jnp.int32, (slots, rows), 0)
     line = lax.broadcasted_iota(jnp.int32, (STATS, rows), 0)
+    lane = lax.rem(lax.broadcasted_iota(jnp.int32, (1, rows), 1), SPAN)
+    core = lax.axis_index("core")
+    chunk = 2 * lax.axis_index("y") + core
+    offsets = (lane - chunk * slots, lane - (chunk + 1 - 2 * core) * slots)
     scale = math.log2(math.e) / math.sqrt(HD)
     for request in range(requests):
         wanted = queries[request]
         scores = []
-        for key, start in zip((keys, other_keys), starts):
+        for key, offset in zip((keys, other_keys), offsets):
             score = lax.dot_general(
                 key[request], wanted, (((1,), (1,)), ((), ())), preferred_element_type=F32
             )
-            scores.append(jnp.where(ahead <= prefix[request] - start, score * scale, MASKED))
+            visible = slot <= prefix[:, request : request + 1] + offset
+            scores.append(jnp.where(visible, score * scale, MASKED))
         peak = jnp.maximum(*[jnp.max(s, axis=0, keepdims=True) for s in scores])
         peak = jnp.maximum(peak, FLOOR).astype(BF16).astype(F32)
         weights = [jnp.exp2(s - peak) for s in scores]
@@ -87,7 +87,8 @@
             out[2 * request + group, pl.ds(HD, STATS), :] = stats[:, part]
 
 
-def combine_kernel(parts, out):
+def combine_kernel(parts, weight, out):
+    del weight
     count = parts.shape[0]
     stats = [parts[i, pl.ds(HD, STATS), :].astype(F32) for i in range(count)]
     peaks = [s[0:1] for s in stats]
@@ -120,19 +121,19 @@
         out[2 * pair + 1] = product[:, HD:]
 
 
-def update_kernel(shares, residual, updated, rounded, squares):
+def update_kernel(shares, residual, updated, squares):
     total = residual[...].astype(F32)
     for i in range(shares.shape[0]):
         total += shares[i].astype(F32)
     updated[...] = total
-    rounded[...] = total.astype(BF16)
     own = jnp.sum(total * total, axis=1, keepdims=True)
     row = jnp.broadcast_to(own, total.shape).T[0:8]
     for i in range(squares.shape[0] // 8):
         squares[pl.ds(8 * i, 8), :] = row
 
 
-def norm_kernel(width, updated, squares, gain, out):
+def norm_kernel(width, updated, squares, gain, rounded, out):
+    rounded[...] = updated[...].astype(BF16)
     total = jnp.sum(squares[...], axis=0, keepdims=True)
     factor = lax.rsqrt(total / width + EPSILON)
     column = jnp.broadcast_to(factor, updated.shape).T
@@ -144,13 +145,8 @@
     pipes = lax.axis_size("pipe")
     devices = 2 * chips * pipes
     tokens = queries.shape[0]
-    slots = cache_keys.shape[1]
     depth, groups, width = out_weight.shape
     weight = out_weight.reshape(depth, groups * width)
-    core = lax.axis_index("core")
-    chip = lax.axis_index("y")
-    place = jnp.stack([(2 * chip + core) * slots, (2 * chip + 1 - core) * slots]).astype(jnp.int32)
-
     gathered = lax.all_to_all(
         jnp.broadcast_to(queries, (chips, tokens, HD)), "y", 0, 0, tiled=True
     )
@@ -169,8 +165,8 @@
     parts = call(
         attend_kernel,
         jax.ShapeDtypeStruct((chips, HD + STATS, HD), BF16),
-        (place, prefix_lengths, arranged, cache_keys, cache_values, other_keys, other_values, weight),
-        in_specs=[SMEM, SMEM] + [VMEM] * 5 + [pl.BlockSpec(memory_space=pl.ANY)],
+        (prefix_lengths.reshape(1, -1), arranged, cache_keys, cache_values, other_keys, other_values),
+        in_specs=[VMEM] * 6,
         flops=4 * 2 * 2 * 512 * 256 * HD,
         moved=2**21,
         name="attend",
@@ -179,7 +175,8 @@
     own = call(
         combine_kernel,
         jax.ShapeDtypeStruct((chips, HD, HD), BF16),
-        (parts,),
+        (parts, weight),
+        in_specs=[VMEM, pl.BlockSpec(memory_space=pl.ANY)],
         flops=2 * 8 * HD * HD,
         moved=2**19,
         name="combine",
@@ -197,11 +194,10 @@
         name="project",
     )
     shares = lax.all_to_all(shares, "pipe", 0, 0, tiled=True)
-    updated, rounded, squares = call(
+    updated, squares = call(
         update_kernel,
         (
             jax.ShapeDtypeStruct((tokens, width), F32),
-            jax.ShapeDtypeStruct((tokens, width), BF16),
             jax.ShapeDtypeStruct((devices, tokens), F32),
         ),
         (shares, residual_in),
@@ -213,15 +209,14 @@
         squares.reshape(devices, 1, tokens), ("pipe", "y", "core"), 0, 0, tiled=True
     ).reshape(devices, tokens)
 
-    normed = call(
+    return call(
         lambda *refs: norm_kernel(devices * width, *refs),
-        jax.ShapeDtypeStruct((tokens, width), BF16),
+        (jax.ShapeDtypeStruct((tokens, width), BF16),) * 2,
         (updated, squares, norm_gain.reshape(1, width)),
         flops=4 * tokens * width,
         moved=2**18,
         name="norm",
     )
-    return rounded, normed
 
 
 def solution(mesh):

time: 81.2 us -> 79.3 us (0.977)
  blocking collectives: 56.7 us -> 38.6 us
  waiting for transfers between devices: 0.84 us -> 12 us
  starting transfers between devices: 14.1 us -> 20.3 us
  Pallas kernels: 4.47 us -> 3.54 us
    all_to_all x1 -> x0, blocking collectives: 18.1 us -> none  [on_device(): parts = lax.all_to_all(parts, 'y', 0, 0, tiled=True)]
    all_to_all x0 -> x1, waiting for transfers between devices: none -> 9.22 us  [on_device(): parts = lax.all_to_all(parts, 'y', 0, 0, tiled=True)]
    all_to_all x0 -> x1, starting transfers between devices: none -> 6.05 us  [on_device(): parts = lax.all_to_all(parts, 'y', 0, 0, tiled=True)]
    all_to_all x1, waiting for transfers between devices: 0.83 us -> 2.75 us  [on_device(): lax.all_to_all(jnp.broadcast_to(queries, (chips, tokens, HD)), 'y', 0, 0,...]
    pallas_call x6, Pallas kernels: 4.47 us -> 3.54 us  [call(): pl.pallas_call(kernel, out_shape=out_shape, in_specs=in_specs or [VMEM] *...]
  transfers between devices with their start and end apart: 3 -> 4, of which waited for: 1 -> 2; matrix products, arithmetic and copies ran while one was open for 3% -> 2% of each run, Pallas kernels for 0% -> 0%
where the time goes in v3:
time: 79.3 us; the launch traced here: 78.7 us
  blocking collectives  38.6 us (49%)
  starting transfers between devices  20.3 us (26%)
  waiting for transfers between devices  12 us (15%)
  Pallas kernels  3.54 us (4%)
  local copies, waits for them, and re-layouts  3.48 us (4%)
    all_to_all x1, blocking collectives, on_device(): lax.all_to_all(squares.reshape(devices, 1, tokens), ('pipe', 'y', 'core')...  14.2 us
    all_to_all x1, blocking collectives, on_device(): half = lax.all_to_all(own, 'y', 0, 0, tiled=True)  11.8 us
    all_to_all x1, waiting for transfers between devices, on_device(): parts = lax.all_to_all(parts, 'y', 0, 0, tiled=True)  9.22 us
    all_to_all x1, starting transfers between devices, on_device(): lax.all_to_all(jnp.broadcast_to(queries, (chips, tokens, HD)), 'y', 0, 0,...  7.65 us
    all_to_all x1, blocking collectives, on_device(): shares = lax.all_to_all(shares, 'pipe', 0, 0, tiled=True)  7.22 us
    all_to_all x1, starting transfers between devices, on_device(): parts = lax.all_to_all(parts, 'y', 0, 0, tiled=True)  6.05 us
    all_gather x1, blocking collectives, on_device(): attended = lax.all_gather(half, 'core')  5.34 us
    ppermute x1, starting transfers between devices, on_device(): other_keys = lax.ppermute(cache_keys, 'core', swap)  4.69 us
  transfers between devices with their start and end apart: 4, of which 2 were waited for; matrix products, arithmetic and copies ran while one was open for 2% of the time, Pallas kernels for 0%

profile of v3, /device:TPU:1, one launch (start us, length us, event | category | flops | bytes accessed | tf_op | source)
XLA Modules:
  0.0 78.7 jit_solution(4790765233568941645)
XLA Ops:
  0.6 1.5 %broadcast_in_dim.3 = bf16[8,128,128]{2,1,0:T(8,128)(2,1)} broadcast(bf16[128,128]{1,0:T(8,128)(2,1)} %param.7), dimensions={1,2} | broadcast | bytes 294912 | tf_op jit(solution)/shard_map/broadcast_in_dim | solution.py:151
  2.1 7.7 %all-to-all-start = ((bf16[8,128,128]{2,1,0:T(8,128)(2,1)}), bf16[8,128,128]{2,1,0:T(8,128)(2,1)S(1)}, u32[]{:S(2)}, u32[]{:S(2)}) async-start(bf16[8,128,128]{2,1,0:T(8,128)(2,1)} %broadcast_in_dim.3), calls=%async_computation | async-start | bytes 524288 | tf_op jit(solution)/shard_map/all_to_all | solution.py:150
  9.8 0.0 copy-start.1
  9.8 0.0 copy-start.3
  9.8 4.7 %collective-permute-start = (bf16[4,256,256]{2,1,0:T(8,128)(2,1)}, bf16[4,256,256]{2,1,0:T(8,128)(2,1)S(1)}, u32[]{:S(2)}, u32[]{:S(2)}) collective-permute-start(bf16[4,256,256]{2,1,0:T(8,128)(2,1)} %keys.1), channel_id=1, source_target_pairs={{0,1},{1,0},{2,3},{3,2},{4,5},{5,4},{6,7},{7,6},{8,9},{9,8},{10,11... | collective-permute-start | bytes 1572872 | tf_op jit(solution)/shard_map/ppermute | solution.py:154
  14.5 1.9 %collective-permute-start.1 = (bf16[4,256,256]{2,1,0:T(8,128)(2,1)}, bf16[4,256,256]{2,1,0:T(8,128)(2,1)S(1)}, u32[]{:S(2)}, u32[]{:S(2)}) collective-permute-start(bf16[4,256,256]{2,1,0:T(8,128)(2,1)} %values.1), channel_id=1, source_target_pairs={{0,1},{1,0},{2,3},{3,2},{4,5},{5,4},{6,7},{7,6},{8,9},{9,8},{10,11... | collective-permute-start | bytes 1572872 | tf_op jit(solution)/shard_map/ppermute | solution.py:155
  16.4 2.7 %all-to-all-done.queries = bf16[8,128,128]{2,1,0:T(8,128)(2,1)S(1)} async-done(((bf16[8,128,128]{2,1,0:T(8,128)(2,1)}), bf16[8,128,128]{2,1,0:T(8,128)(2,1)S(1)}, u32[]{:S(2)}, u32[]{:S(2)}) %all-to-all-start) | async-done | bytes 262176 | tf_op jit(solution)/shard_map/all_to_all | solution.py:150
  19.2 0.1 arrange.1.queries
  19.3 0.0 collective-permute-done.other_keys
  19.3 0.0 collective-permute-done.1.other_values
  19.3 0.0 copy-done
  19.3 2.0 %attend.1 = bf16[8,144,128]{2,1,0:T(8,128)(2,1)} custom-call(s32[1,4]{1,0:T(1,128)S(1)} %bitcast.16, bf16[4,256,256]{2,1,0:T(8,128)(2,1)S(1)} %arrange.1.queries, bf16[4,256,256]{2,1,0:T(8,128)(2,1)S(1)} %copy-done, bf16[4,256,256]{2,1,0:T(8,128)(2,1)S(1)} %copy-done.1, bf16[4,256,256]{2,1,0:T(8,128)(2,1)S(1)} %collective-permute-done.other_keys, ...), custom_call_target="tpu_custom_call" | custom-call | flops 268435456 | bytes 2097152 | tf_op jit(solution)/shard_map/attend/pallas_call | solution.py:24
  21.3 6.0 %all-to-all-start.1 = ((bf16[8,144,128]{2,1,0:T(8,128)(2,1)}), bf16[8,144,128]{2,1,0:T(8,128)(2,1)S(1)}, u32[]{:S(2)}, u32[]{:S(2)}) async-start(bf16[8,144,128]{2,1,0:T(8,128)(2,1)} %attend.1), calls=%async_computation.1 | async-start | bytes 589824 | tf_op jit(solution)/shard_map/all_to_all | solution.py:174
  27.3 2.0 %copy.12 = bf16[256,8,4,128]{3,1,2,0:T(8,128)(2,1)S(1)} copy(bf16[256,8,4,128]{3,2,1,0:T(4,128)(2,1)} %bitcast.18) | data formatting | bytes 4194304
  29.3 9.2 %all-to-all-done.1.parts = bf16[8,144,128]{2,1,0:T(8,128)(2,1)S(1)} async-done(((bf16[8,144,128]{2,1,0:T(8,128)(2,1)}), bf16[8,144,128]{2,1,0:T(8,128)(2,1)S(1)}, u32[]{:S(2)}, u32[]{:S(2)}) %all-to-all-start.1) | async-done | bytes 294944 | tf_op jit(solution)/shard_map/all_to_all | solution.py:174
  38.5 0.2 combine.1
  38.7 0.0 copy-start.2
  38.7 11.8 %all_to_all.25 = bf16[8,128,128]{2,1,0:T(8,128)(2,1)S(1)} all-to-all(bf16[8,128,128]{2,1,0:T(8,128)(2,1)S(1)} %combine.1), channel_id=1, replica_groups=mesh['replica'=8,'pipe'=4,'y'=8,'core'=2] {'y'}, dimensions={0} | all-to-all | bytes 524288 | tf_op jit(solution)/shard_map/all_to_all | solution.py:184
  50.5 5.3 %all-gather = bf16[16,128,128]{2,1,0:T(8,128)(2,1)S(1)} all-gather(bf16[8,128,128]{2,1,0:T(8,128)(2,1)S(1)} %all_to_all.25), channel_id=2, replica_groups=mesh['replica'=8,'pipe'=4,'y'=8,'core'=2] {'core'}, dimensions={0}, use_global_device_ids=true | all-gather | bytes 786432 | tf_op jit(solution)/shard_map/all_gather | solution.py:185
  55.9 0.5 project.1
  56.3 7.2 %all_to_all.26.shares = bf16[4,128,128]{2,1,0:T(8,128)(2,1)S(1)} all-to-all(bf16[4,128,128]{2,1,0:T(8,128)(2,1)S(1)} %project.1), channel_id=1, replica_groups=mesh['replica'=8,'pipe'=4,'y'=8,'core'=2] {'pipe'}, dimensions={0} | all-to-all | bytes 262144 | tf_op jit(solution)/shard_map/all_to_all | solution.py:196
  63.6 0.1 update.1
  63.7 14.2 %all_to_all.27 = f32[64,1,128]{2,1,0:T(1,128)S(1)} all-to-all(f32[64,1,128]{2,1,0:T(1,128)S(1)} %bitcast.15), channel_id=1, replica_groups=mesh['replica'=8,'pipe'=4,'y'=8,'core'=2] {'pipe','y','core'}, dimensions={0} | all-to-all | bytes 65536 | tf_op jit(solution)/shard_map/all_to_all | solution.py:208
  77.9 0.7 norm.1
  (6 shorter events, 0.0 us)
Async XLA Ops:
  2.1 17.1 %all-to-all-start = ((bf16[8,128,128]{2,1,0:T(8,128)(2,1)}), bf16[8,128,128]{2,1,0:T(8,128)(2,1)S(1)}, u32[]{:S(2)}, u32[]{:S(2)}) async-start(bf16[8,128,128]{2,1,0:T(8,128)(2,1)} %broadcast_in_dim.3), calls=%async_computation | async-start | bytes 524288 | tf_op jit(solution)/shard_map/all_to_all | solution.py:150
  9.8 9.5 %copy-start = (bf16[4,256,256]{2,1,0:T(8,128)(2,1)S(1)}, bf16[4,256,256]{2,1,0:T(8,128)(2,1)}, u32[]{:S(2)}) copy-start(bf16[4,256,256]{2,1,0:T(8,128)(2,1)} %keys.1) | copy-start | bytes 1572868
  9.8 9.5 %copy-start.1 = (bf16[4,256,256]{2,1,0:T(8,128)(2,1)S(1)}, bf16[4,256,256]{2,1,0:T(8,128)(2,1)}, u32[]{:S(2)}) copy-start(bf16[4,256,256]{2,1,0:T(8,128)(2,1)} %values.1) | copy-start | bytes 1572868
  9.8 9.5 %copy-start.3 = (s32[4]{0:T(128)S(1)}, s32[4]{0:T(128)}, u32[]{:S(2)}) copy-start(s32[4]{0:T(128)} %param.10) | copy-start | bytes 52
  9.8 9.5 %collective-permute-start = (bf16[4,256,256]{2,1,0:T(8,128)(2,1)}, bf16[4,256,256]{2,1,0:T(8,128)(2,1)S(1)}, u32[]{:S(2)}, u32[]{:S(2)}) collective-permute-start(bf16[4,256,256]{2,1,0:T(8,128)(2,1)} %keys.1), channel_id=1, source_target_pairs={{0,1},{1,0},{2,3},{3,2},{4,5},{5,4},{6,7},{7,6},{8,9},{9,8},{10,11... | collective-permute-start | bytes 1572872 | tf_op jit(solution)/shard_map/ppermute | solution.py:154
  14.5 4.8 %collective-permute-start.1 = (bf16[4,256,256]{2,1,0:T(8,128)(2,1)}, bf16[4,256,256]{2,1,0:T(8,128)(2,1)S(1)}, u32[]{:S(2)}, u32[]{:S(2)}) collective-permute-start(bf16[4,256,256]{2,1,0:T(8,128)(2,1)} %values.1), channel_id=1, source_target_pairs={{0,1},{1,0},{2,3},{3,2},{4,5},{5,4},{6,7},{7,6},{8,9},{9,8},{10,11... | collective-permute-start | bytes 1572872 | tf_op jit(solution)/shard_map/ppermute | solution.py:155
  21.3 17.2 %all-to-all-start.1 = ((bf16[8,144,128]{2,1,0:T(8,128)(2,1)}), bf16[8,144,128]{2,1,0:T(8,128)(2,1)S(1)}, u32[]{:S(2)}, u32[]{:S(2)}) async-start(bf16[8,144,128]{2,1,0:T(8,128)(2,1)} %attend.1), calls=%async_computation.1 | async-start | bytes 589824 | tf_op jit(solution)/shard_map/all_to_all | solution.py:174
  38.7 24.9 %copy-start.2 = (bf16[128,128]{1,0:T(8,128)(2,1)S(1)}, bf16[128,128]{1,0:T(8,128)(2,1)}, u32[]{:S(2)}) copy-start(bf16[128,128]{1,0:T(8,128)(2,1)} %residual.1) | copy-start | bytes 98308
  50.5 27.4 %copy-start.4 = (f32[128]{0:T(128)S(1)}, f32[128]{0:T(128)}, u32[]{:S(2)}) copy-start(f32[128]{0:T(128)} %param.13) | copy-start | bytes 1540

commit v4 on v3

--- a/solution.py
+++ b/solution.py
@@ -20,12 +20,12 @@
 BF16 = jnp.bfloat16
 
 
-def call(kernel, out_shape, args, in_specs=None, scratch=(), flops=0, moved=0, name=None):
+def call(kernel, out_shape, args, in_specs=None, out_specs=None, scratch=(), flops=0, moved=0, name=None):
     return pl.pallas_call(
         kernel,
         out_shape=out_shape,
         in_specs=in_specs or [VMEM] * len(args),
-        out_specs=jax.tree.map(lambda _: VMEM, out_shape),
+        out_specs=out_specs or jax.tree.map(lambda _: VMEM, out_shape),
         scratch_shapes=list(scratch),
         compiler_params=pltpu.CompilerParams(vmem_limit_bytes=24 * 2**20),
         cost_estimate=pl.CostEstimate(flops=flops, bytes_accessed=moved, transcendentals=0),
@@ -47,7 +47,7 @@
                 )
 
 
-def attend_kernel(prefix, queries, keys, values, other_keys, other_values, out):
+def attend_kernel(prefix, queries, keys, values, other_keys, other_values, out, staged, sems):
     requests, slots, width = keys.shape
     rows = width
     slot = lax.broadcasted_iota(jnp.int32, (slots, rows), 0)
@@ -57,6 +57,7 @@
     chunk = 2 * lax.axis_index("y") + core
     offsets = (lane - chunk * slots, lane - (chunk + 1 - 2 * core) * slots)
     scale = math.log2(math.e) / math.sqrt(HD)
+    copies = []
     for request in range(requests):
         wanted = queries[request]
         scores = []
@@ -83,8 +84,13 @@
         ).astype(BF16)
         for group in range(2):
             part = slice(group * HD, (group + 1) * HD)
-            out[2 * request + group, pl.ds(0, HD), :] = (summed[part, part] * inverse[:, part]).astype(BF16)
-            out[2 * request + group, pl.ds(HD, STATS), :] = stats[:, part]
+            staged[2 * request + group, pl.ds(0, HD), :] = (summed[part, part] * inverse[:, part]).astype(BF16)
+            staged[2 * request + group, pl.ds(HD, STATS), :] = stats[:, part]
+        pair = pl.ds(2 * request, 2)
+        copies.append(pltpu.make_async_copy(staged.at[pair], out.at[pair], sems.at[request]))
+        copies[-1].start()
+    for copy in copies:
+        copy.wait()
 
 
 def combine_kernel(parts, weight, out):
@@ -166,7 +172,11 @@
         attend_kernel,
         jax.ShapeDtypeStruct((chips, HD + STATS, HD), BF16),
         (prefix_lengths.reshape(1, -1), arranged, cache_keys, cache_values, other_keys, other_values),
-        in_specs=[VMEM] * 6,
+        out_specs=pl.BlockSpec(memory_space=pl.ANY),
+        scratch=[
+            pltpu.VMEM((chips, HD + STATS, HD), BF16),
+            pltpu.SemaphoreType.DMA((cache_keys.shape[0],)),
+        ],
         flops=4 * 2 * 2 * 512 * 256 * HD,
         moved=2**21,
         name="attend",

time: 79.3 us -> 79.3 us (level)
  no operation moved by 1% of the time
where the time goes in v4:
time: 79.3 us; the launch traced here: 78.6 us
  blocking collectives  38.6 us (49%)
  starting transfers between devices  20.3 us (26%)
  waiting for transfers between devices  12 us (15%)
  local copies, waits for them, and re-layouts  3.48 us (4%)
  Pallas kernels  3.45 us (4%)
    all_to_all x1, blocking collectives, on_device(): lax.all_to_all(squares.reshape(devices, 1, tokens), ('pipe', 'y', 'core')...  14.2 us
    all_to_all x1, blocking collectives, on_device(): half = lax.all_to_all(own, 'y', 0, 0, tiled=True)  11.8 us
    all_to_all x1, waiting for transfers between devices, on_device(): parts = lax.all_to_all(parts, 'y', 0, 0, tiled=True)  9.22 us
    all_to_all x1, starting transfers between devices, on_device(): lax.all_to_all(jnp.broadcast_to(queries, (chips, tokens, HD)), 'y', 0, 0,...  7.65 us
    all_to_all x1, blocking collectives, on_device(): shares = lax.all_to_all(shares, 'pipe', 0, 0, tiled=True)  7.22 us
    all_to_all x1, starting transfers between devices, on_device(): parts = lax.all_to_all(parts, 'y', 0, 0, tiled=True)  6.06 us
    all_gather x1, blocking collectives, on_device(): attended = lax.all_gather(half, 'core')  5.34 us
    ppermute x1, starting transfers between devices, on_device(): other_keys = lax.ppermute(cache_keys, 'core', swap)  4.69 us
  transfers between devices with their start and end apart: 4, of which 2 were waited for; matrix products, arithmetic and copies ran while one was open for 2% of the time, Pallas kernels for 0%

profile of v4, /device:TPU:1, one launch (start us, length us, event | category | flops | bytes accessed | tf_op | source)
XLA Modules:
  0.0 78.6 jit_solution(17010909961279224200)
XLA Ops:
  0.6 1.5 %broadcast_in_dim.3 = bf16[8,128,128]{2,1,0:T(8,128)(2,1)} broadcast(bf16[128,128]{1,0:T(8,128)(2,1)} %param.7), dimensions={1,2} | broadcast | bytes 294912 | tf_op jit(solution)/shard_map/broadcast_in_dim | solution.py:157
  2.1 7.7 %all-to-all-start = ((bf16[8,128,128]{2,1,0:T(8,128)(2,1)}), bf16[8,128,128]{2,1,0:T(8,128)(2,1)S(1)}, u32[]{:S(2)}, u32[]{:S(2)}) async-start(bf16[8,128,128]{2,1,0:T(8,128)(2,1)} %broadcast_in_dim.3), calls=%async_computation | async-start | bytes 524288 | tf_op jit(solution)/shard_map/all_to_all | solution.py:156
  9.8 0.0 copy-start.1
  9.8 0.0 copy-start.3
  9.8 4.7 %collective-permute-start = (bf16[4,256,256]{2,1,0:T(8,128)(2,1)}, bf16[4,256,256]{2,1,0:T(8,128)(2,1)S(1)}, u32[]{:S(2)}, u32[]{:S(2)}) collective-permute-start(bf16[4,256,256]{2,1,0:T(8,128)(2,1)} %keys.1), channel_id=1, source_target_pairs={{0,1},{1,0},{2,3},{3,2},{4,5},{5,4},{6,7},{7,6},{8,9},{9,8},{10,11... | collective-permute-start | bytes 1572872 | tf_op jit(solution)/shard_map/ppermute | solution.py:160
  14.5 1.9 %collective-permute-start.1 = (bf16[4,256,256]{2,1,0:T(8,128)(2,1)}, bf16[4,256,256]{2,1,0:T(8,128)(2,1)S(1)}, u32[]{:S(2)}, u32[]{:S(2)}) collective-permute-start(bf16[4,256,256]{2,1,0:T(8,128)(2,1)} %values.1), channel_id=1, source_target_pairs={{0,1},{1,0},{2,3},{3,2},{4,5},{5,4},{6,7},{7,6},{8,9},{9,8},{10,11... | collective-permute-start | bytes 1572872 | tf_op jit(solution)/shard_map/ppermute | solution.py:161
  16.4 2.7 %all-to-all-done.queries = bf16[8,128,128]{2,1,0:T(8,128)(2,1)S(1)} async-done(((bf16[8,128,128]{2,1,0:T(8,128)(2,1)}), bf16[8,128,128]{2,1,0:T(8,128)(2,1)S(1)}, u32[]{:S(2)}, u32[]{:S(2)}) %all-to-all-start) | async-done | bytes 262176 | tf_op jit(solution)/shard_map/all_to_all | solution.py:156
  19.2 0.1 arrange.1.queries
  19.3 0.0 collective-permute-done.other_keys
  19.3 0.0 collective-permute-done.1.other_values
  19.3 1.9 %attend.1 = bf16[8,144,128]{2,1,0:T(8,128)(2,1)} custom-call(s32[1,4]{1,0:T(1,128)S(1)} %bitcast.16, bf16[4,256,256]{2,1,0:T(8,128)(2,1)S(1)} %arrange.1.queries, bf16[4,256,256]{2,1,0:T(8,128)(2,1)S(1)} %copy-done, bf16[4,256,256]{2,1,0:T(8,128)(2,1)S(1)} %copy-done.1, bf16[4,256,256]{2,1,0:T(8,128)(2,1)S(1)} %collective-permute-done.other_keys, ...), custom_call_target="tpu_custom_call" | custom-call | flops 268435456 | bytes 2097152 | tf_op jit(solution)/shard_map/attend/pallas_call | solution.py:24
  21.2 6.1 %all-to-all-start.1 = ((bf16[8,144,128]{2,1,0:T(8,128)(2,1)}), bf16[8,144,128]{2,1,0:T(8,128)(2,1)S(1)}, u32[]{:S(2)}, u32[]{:S(2)}) async-start(bf16[8,144,128]{2,1,0:T(8,128)(2,1)} %attend.1), calls=%async_computation.1 | async-start | bytes 589824 | tf_op jit(solution)/shard_map/all_to_all | solution.py:184
  27.3 2.0 %copy.12 = bf16[256,8,4,128]{3,1,2,0:T(8,128)(2,1)S(1)} copy(bf16[256,8,4,128]{3,2,1,0:T(4,128)(2,1)} %bitcast.18) | data formatting | bytes 4194304
  29.2 9.2 %all-to-all-done.1.parts = bf16[8,144,128]{2,1,0:T(8,128)(2,1)S(1)} async-done(((bf16[8,144,128]{2,1,0:T(8,128)(2,1)}), bf16[8,144,128]{2,1,0:T(8,128)(2,1)S(1)}, u32[]{:S(2)}, u32[]{:S(2)}) %all-to-all-start.1) | async-done | bytes 294944 | tf_op jit(solution)/shard_map/all_to_all | solution.py:184
  38.4 0.2 combine.1
  38.6 0.0 copy-start.2
  38.6 11.8 %all_to_all.25 = bf16[8,128,128]{2,1,0:T(8,128)(2,1)S(1)} all-to-all(bf16[8,128,128]{2,1,0:T(8,128)(2,1)S(1)} %combine.1), channel_id=1, replica_groups=mesh['replica'=8,'pipe'=4,'y'=8,'core'=2] {'y'}, dimensions={0} | all-to-all | bytes 524288 | tf_op jit(solution)/shard_map/all_to_all | solution.py:194
  50.4 5.3 %all-gather = bf16[16,128,128]{2,1,0:T(8,128)(2,1)S(1)} all-gather(bf16[8,128,128]{2,1,0:T(8,128)(2,1)S(1)} %all_to_all.25), channel_id=2, replica_groups=mesh['replica'=8,'pipe'=4,'y'=8,'core'=2] {'core'}, dimensions={0}, use_global_device_ids=true | all-gather | bytes 786432 | tf_op jit(solution)/shard_map/all_gather | solution.py:195
  55.8 0.5 project.1
  56.3 7.2 %all_to_all.26.shares = bf16[4,128,128]{2,1,0:T(8,128)(2,1)S(1)} all-to-all(bf16[4,128,128]{2,1,0:T(8,128)(2,1)S(1)} %project.1), channel_id=1, replica_groups=mesh['replica'=8,'pipe'=4,'y'=8,'core'=2] {'pipe'}, dimensions={0} | all-to-all | bytes 262144 | tf_op jit(solution)/shard_map/all_to_all | solution.py:206
  63.5 0.0 copy-done.2
  63.5 0.1 update.1
  63.6 14.2 %all_to_all.27 = f32[64,1,128]{2,1,0:T(1,128)S(1)} all-to-all(f32[64,1,128]{2,1,0:T(1,128)S(1)} %bitcast.15), channel_id=1, replica_groups=mesh['replica'=8,'pipe'=4,'y'=8,'core'=2] {'pipe','y','core'}, dimensions={0} | all-to-all | bytes 65536 | tf_op jit(solution)/shard_map/all_to_all | solution.py:218
  77.9 0.7 norm.1
  (6 shorter events, 0.0 us)
Async XLA Ops:
  2.1 17.1 %all-to-all-start = ((bf16[8,128,128]{2,1,0:T(8,128)(2,1)}), bf16[8,128,128]{2,1,0:T(8,128)(2,1)S(1)}, u32[]{:S(2)}, u32[]{:S(2)}) async-start(bf16[8,128,128]{2,1,0:T(8,128)(2,1)} %broadcast_in_dim.3), calls=%async_computation | async-start | bytes 524288 | tf_op jit(solution)/shard_map/all_to_all | solution.py:156
  9.8 9.5 %copy-start = (bf16[4,256,256]{2,1,0:T(8,128)(2,1)S(1)}, bf16[4,256,256]{2,1,0:T(8,128)(2,1)}, u32[]{:S(2)}) copy-start(bf16[4,256,256]{2,1,0:T(8,128)(2,1)} %keys.1) | copy-start | bytes 1572868
  9.8 9.5 %copy-start.1 = (bf16[4,256,256]{2,1,0:T(8,128)(2,1)S(1)}, bf16[4,256,256]{2,1,0:T(8,128)(2,1)}, u32[]{:S(2)}) copy-start(bf16[4,256,256]{2,1,0:T(8,128)(2,1)} %values.1) | copy-start | bytes 1572868
  9.8 9.5 %copy-start.3 = (s32[4]{0:T(128)S(1)}, s32[4]{0:T(128)}, u32[]{:S(2)}) copy-start(s32[4]{0:T(128)} %param.10) | copy-start | bytes 52
  9.8 9.5 %collective-permute-start = (bf16[4,256,256]{2,1,0:T(8,128)(2,1)}, bf16[4,256,256]{2,1,0:T(8,128)(2,1)S(1)}, u32[]{:S(2)}, u32[]{:S(2)}) collective-permute-start(bf16[4,256,256]{2,1,0:T(8,128)(2,1)} %keys.1), channel_id=1, source_target_pairs={{0,1},{1,0},{2,3},{3,2},{4,5},{5,4},{6,7},{7,6},{8,9},{9,8},{10,11... | collective-permute-start | bytes 1572872 | tf_op jit(solution)/shard_map/ppermute | solution.py:160
  14.5 4.8 %collective-permute-start.1 = (bf16[4,256,256]{2,1,0:T(8,128)(2,1)}, bf16[4,256,256]{2,1,0:T(8,128)(2,1)S(1)}, u32[]{:S(2)}, u32[]{:S(2)}) collective-permute-start(bf16[4,256,256]{2,1,0:T(8,128)(2,1)} %values.1), channel_id=1, source_target_pairs={{0,1},{1,0},{2,3},{3,2},{4,5},{5,4},{6,7},{7,6},{8,9},{9,8},{10,11... | collective-permute-start | bytes 1572872 | tf_op jit(solution)/shard_map/ppermute | solution.py:161
  21.2 17.2 %all-to-all-start.1 = ((bf16[8,144,128]{2,1,0:T(8,128)(2,1)}), bf16[8,144,128]{2,1,0:T(8,128)(2,1)S(1)}, u32[]{:S(2)}, u32[]{:S(2)}) async-start(bf16[8,144,128]{2,1,0:T(8,128)(2,1)} %attend.1), calls=%async_computation.1 | async-start | bytes 589824 | tf_op jit(solution)/shard_map/all_to_all | solution.py:184
  38.6 24.9 %copy-start.2 = (bf16[128,128]{1,0:T(8,128)(2,1)S(1)}, bf16[128,128]{1,0:T(8,128)(2,1)}, u32[]{:S(2)}) copy-start(bf16[128,128]{1,0:T(8,128)(2,1)} %residual.1) | copy-start | bytes 98308
  50.4 27.4 %copy-start.4 = (f32[128]{0:T(128)S(1)}, f32[128]{0:T(128)}, u32[]{:S(2)}) copy-start(f32[128]{0:T(128)} %param.13) | copy-start | bytes 1540

commit v5 on v4

--- a/solution.py
+++ b/solution.py
@@ -111,7 +111,11 @@
         out[i] = attended
 
 
-def project_kernel(attended, weight, out, joined):
+def project_kernel(attended, weight, residual, out, own, joined):
+    pipe = lax.axis_index("pipe")
+    width = residual.shape[1]
+    added = residual[...].astype(F32)
+    mine = added
     for core in range(2):
         for place in range(attended.shape[1]):
             request, group = place // 2, place % 2
@@ -121,19 +125,35 @@
                 ] = attended[core, place, pl.ds(SPAN * j, SPAN), :]
     for pair in range(2):
         product = jnp.dot(
-            joined[...], weight[:, pl.ds(2 * HD * pair, 2 * HD)], preferred_element_type=F32
-        ).astype(BF16)
-        out[2 * pair] = product[:, :HD]
-        out[2 * pair + 1] = product[:, HD:]
-
-
-def update_kernel(shares, residual, updated, squares):
-    total = residual[...].astype(F32)
+            joined[...], weight[:, pl.ds(2 * width * pair, 2 * width)], preferred_element_type=F32
+        )
+        for of in range(2):
+            group = 2 * pair + of
+            share = product[:, of * width : (of + 1) * width].astype(BF16).astype(F32)
+            here = jnp.where(pipe == group, 1.0, 0.0)
+            mine += share * here
+            sent = (share + added * here).astype(BF16)
+            for to in range(out.shape[0]):
+                out[to, :, pl.ds(group * width, width)] = sent
+    own[...] = mine
+
+
+def update_kernel(shares, own, updated, squares):
+    pipe = lax.axis_index("pipe")
+    width = own.shape[1]
+    total = own[...]
+    square = jnp.zeros_like(total)
     for i in range(shares.shape[0]):
-        total += shares[i].astype(F32)
+        away = jnp.where(pipe == i, 0.0, 1.0)
+        block = pl.ds(pl.multiple_of(pipe * width, width), width)
+        total += shares[i, :, block].astype(F32) * away
+        other = sum(
+            shares[j, :, pl.ds(i * width, width)].astype(F32) for j in range(shares.shape[0])
+        )
+        square += other * other * away
     updated[...] = total
-    own = jnp.sum(total * total, axis=1, keepdims=True)
-    row = jnp.broadcast_to(own, total.shape).T[0:8]
+    square = jnp.sum(square + total * total, axis=1, keepdims=True)
+    row = jnp.broadcast_to(square, total.shape).T[0:8]
     for i in range(squares.shape[0] // 8):
         squares[pl.ds(8 * i, 8), :] = row
 
@@ -194,10 +214,13 @@
     half = lax.all_to_all(own, "y", 0, 0, tiled=True)
     attended = lax.all_gather(half, "core")
 
-    shares = call(
+    shares, own = call(
         project_kernel,
-        jax.ShapeDtypeStruct((groups, tokens, width), BF16),
-        (attended.reshape(2, chips, HD, HD), weight),
+        (
+            jax.ShapeDtypeStruct((pipes, tokens, groups * width), BF16),
+            jax.ShapeDtypeStruct((tokens, width), F32),
+        ),
+        (attended.reshape(2, chips, HD, HD), weight, residual_in),
         scratch=[pltpu.VMEM((tokens, depth), BF16)],
         flops=2 * tokens * depth * groups * width,
         moved=3 * 2**20,
@@ -208,16 +231,16 @@
         update_kernel,
         (
             jax.ShapeDtypeStruct((tokens, width), F32),
-            jax.ShapeDtypeStruct((devices, tokens), F32),
+            jax.ShapeDtypeStruct((2 * chips, tokens), F32),
         ),
-        (shares, residual_in),
+        (shares, own),
         flops=8 * tokens * width,
         moved=2**18,
         name="update",
     )
     squares = lax.all_to_all(
-        squares.reshape(devices, 1, tokens), ("pipe", "y", "core"), 0, 0, tiled=True
-    ).reshape(devices, tokens)
+        squares.reshape(2 * chips, 1, tokens), ("y", "core"), 0, 0, tiled=True
+    ).reshape(2 * chips, tokens)
 
     return call(
         lambda *refs: norm_kernel(devices * width, *refs),

time: 79.3 us -> 80 us (level)
    all_to_all x1, blocking collectives: 7.22 us -> 11.5 us  [on_device(): shares = lax.all_to_all(shares, 'pipe', 0, 0, tiled=True)]
    all_to_all x1, blocking collectives: 14.2 us -> 10.8 us  [on_device(): lax.all_to_all(squares.reshape(2 * chips, 1, tokens), ('y', 'core'), 0, 0...]
where the time goes in v5:
time: 80 us; the launch traced here: 79.4 us
  blocking collectives  39.3 us (49%)
  starting transfers between devices  20.3 us (25%)
  waiting for transfers between devices  12 us (15%)
  Pallas kernels  3.57 us (4%)
  local copies, waits for them, and re-layouts  3.48 us (4%)
    all_to_all x1, blocking collectives, on_device(): half = lax.all_to_all(own, 'y', 0, 0, tiled=True)  11.8 us
    all_to_all x1, blocking collectives, on_device(): shares = lax.all_to_all(shares, 'pipe', 0, 0, tiled=True)  11.5 us
    all_to_all x1, blocking collectives, on_device(): lax.all_to_all(squares.reshape(2 * chips, 1, tokens), ('y', 'core'), 0, 0...  10.8 us
    all_to_all x1, waiting for transfers between devices, on_device(): parts = lax.all_to_all(parts, 'y', 0, 0, tiled=True)  9.2 us
    all_to_all x1, starting transfers between devices, on_device(): lax.all_to_all(jnp.broadcast_to(queries, (chips, tokens, HD)), 'y', 0, 0,...  7.65 us
    all_to_all x1, starting transfers between devices, on_device(): parts = lax.all_to_all(parts, 'y', 0, 0, tiled=True)  6.06 us
    all_gather x1, blocking collectives, on_device(): attended = lax.all_gather(half, 'core')  5.2 us
    ppermute x1, starting transfers between devices, on_device(): other_keys = lax.ppermute(cache_keys, 'core', swap)  4.69 us
  transfers between devices with their start and end apart: 4, of which 2 were waited for; matrix products, arithmetic and copies ran while one was open for 2% of the time, Pallas kernels for 0%

profile of v5, /device:TPU:1, one launch (start us, length us, event | category | flops | bytes accessed | tf_op | source)
XLA Modules:
  0.0 79.4 jit_solution(7015549111614523561)
XLA Ops:
  0.6 1.5 %broadcast_in_dim.3 = bf16[8,128,128]{2,1,0:T(8,128)(2,1)} broadcast(bf16[128,128]{1,0:T(8,128)(2,1)} %param.7), dimensions={1,2} | broadcast | bytes 294912 | tf_op jit(solution)/shard_map/broadcast_in_dim | solution.py:177
  2.1 7.7 %all-to-all-start = ((bf16[8,128,128]{2,1,0:T(8,128)(2,1)}), bf16[8,128,128]{2,1,0:T(8,128)(2,1)S(1)}, u32[]{:S(2)}, u32[]{:S(2)}) async-start(bf16[8,128,128]{2,1,0:T(8,128)(2,1)} %broadcast_in_dim.3), calls=%async_computation | async-start | bytes 524288 | tf_op jit(solution)/shard_map/all_to_all | solution.py:176
  9.8 0.0 copy-start.1
  9.8 0.0 copy-start.3
  9.8 4.7 %collective-permute-start = (bf16[4,256,256]{2,1,0:T(8,128)(2,1)}, bf16[4,256,256]{2,1,0:T(8,128)(2,1)S(1)}, u32[]{:S(2)}, u32[]{:S(2)}) collective-permute-start(bf16[4,256,256]{2,1,0:T(8,128)(2,1)} %keys.1), channel_id=1, source_target_pairs={{0,1},{1,0},{2,3},{3,2},{4,5},{5,4},{6,7},{7,6},{8,9},{9,8},{10,11... | collective-permute-start | bytes 1572872 | tf_op jit(solution)/shard_map/ppermute | solution.py:180
  14.5 1.9 %collective-permute-start.1 = (bf16[4,256,256]{2,1,0:T(8,128)(2,1)}, bf16[4,256,256]{2,1,0:T(8,128)(2,1)S(1)}, u32[]{:S(2)}, u32[]{:S(2)}) collective-permute-start(bf16[4,256,256]{2,1,0:T(8,128)(2,1)} %values.1), channel_id=1, source_target_pairs={{0,1},{1,0},{2,3},{3,2},{4,5},{5,4},{6,7},{7,6},{8,9},{9,8},{10,11... | collective-permute-start | bytes 1572872 | tf_op jit(solution)/shard_map/ppermute | solution.py:181
  16.4 2.7 %all-to-all-done.queries = bf16[8,128,128]{2,1,0:T(8,128)(2,1)S(1)} async-done(((bf16[8,128,128]{2,1,0:T(8,128)(2,1)}), bf16[8,128,128]{2,1,0:T(8,128)(2,1)S(1)}, u32[]{:S(2)}, u32[]{:S(2)}) %all-to-all-start) | async-done | bytes 262176 | tf_op jit(solution)/shard_map/all_to_all | solution.py:176
  19.2 0.1 arrange.1.queries
  19.3 0.0 collective-permute-done.other_keys
  19.3 0.0 collective-permute-done.1.other_values
  19.3 1.9 %attend.1 = bf16[8,144,128]{2,1,0:T(8,128)(2,1)} custom-call(s32[1,4]{1,0:T(1,128)S(1)} %bitcast.16, bf16[4,256,256]{2,1,0:T(8,128)(2,1)S(1)} %arrange.1.queries, bf16[4,256,256]{2,1,0:T(8,128)(2,1)S(1)} %copy-done, bf16[4,256,256]{2,1,0:T(8,128)(2,1)S(1)} %copy-done.1, bf16[4,256,256]{2,1,0:T(8,128)(2,1)S(1)} %collective-permute-done.other_keys, ...), custom_call_target="tpu_custom_call" | custom-call | flops 268435456 | bytes 2097152 | tf_op jit(solution)/shard_map/attend/pallas_call | solution.py:24
  21.2 6.1 %all-to-all-start.1 = ((bf16[8,144,128]{2,1,0:T(8,128)(2,1)}), bf16[8,144,128]{2,1,0:T(8,128)(2,1)S(1)}, u32[]{:S(2)}, u32[]{:S(2)}) async-start(bf16[8,144,128]{2,1,0:T(8,128)(2,1)} %attend.1), calls=%async_computation.1 | async-start | bytes 589824 | tf_op jit(solution)/shard_map/all_to_all | solution.py:204
  27.3 2.0 %copy.12 = bf16[256,8,4,128]{3,1,2,0:T(8,128)(2,1)S(1)} copy(bf16[256,8,4,128]{3,2,1,0:T(4,128)(2,1)} %bitcast.18) | data formatting | bytes 4194304
  29.2 0.0 copy-start.2
  29.2 9.2 %all-to-all-done.1.parts = bf16[8,144,128]{2,1,0:T(8,128)(2,1)S(1)} async-done(((bf16[8,144,128]{2,1,0:T(8,128)(2,1)}), bf16[8,144,128]{2,1,0:T(8,128)(2,1)S(1)}, u32[]{:S(2)}, u32[]{:S(2)}) %all-to-all-start.1) | async-done | bytes 294944 | tf_op jit(solution)/shard_map/all_to_all | solution.py:204
  38.4 0.2 combine.1
  38.6 11.8 %all_to_all.25 = bf16[8,128,128]{2,1,0:T(8,128)(2,1)S(1)} all-to-all(bf16[8,128,128]{2,1,0:T(8,128)(2,1)S(1)} %combine.1), channel_id=1, replica_groups=mesh['replica'=8,'pipe'=4,'y'=8,'core'=2] {'y'}, dimensions={0} | all-to-all | bytes 524288 | tf_op jit(solution)/shard_map/all_to_all | solution.py:214
  50.4 5.2 %all-gather = bf16[16,128,128]{2,1,0:T(8,128)(2,1)S(1)} all-gather(bf16[8,128,128]{2,1,0:T(8,128)(2,1)S(1)} %all_to_all.25), channel_id=2, replica_groups=mesh['replica'=8,'pipe'=4,'y'=8,'core'=2] {'core'}, dimensions={0}, use_global_device_ids=true | all-gather | bytes 786432 | tf_op jit(solution)/shard_map/all_gather | solution.py:215
  55.6 0.0 copy-done.2
  55.6 0.5 project.1
  56.2 11.5 %all_to_all.26.shares = bf16[4,128,512]{2,1,0:T(8,128)(2,1)S(1)} all-to-all(bf16[4,128,512]{2,1,0:T(8,128)(2,1)S(1)} %get-tuple-element.6), channel_id=1, replica_groups=mesh['replica'=8,'pipe'=4,'y'=8,'core'=2] {'pipe'}, dimensions={0} | all-to-all | bytes 1048576 | tf_op jit(solution)/shard_map/all_to_all | solution.py:229
  67.7 0.2 update.1
  67.9 10.8 %all_to_all.27 = f32[16,1,128]{2,1,0:T(1,128)S(1)} all-to-all(f32[16,1,128]{2,1,0:T(1,128)S(1)} %bitcast.15), channel_id=1, replica_groups=mesh['replica'=8,'pipe'=4,'y'=8,'core'=2] {'y','core'}, dimensions={0} | all-to-all | bytes 16384 | tf_op jit(solution)/shard_map/all_to_all | solution.py:241
  78.7 0.7 norm.1
  (6 shorter events, 0.0 us)
Async XLA Ops:
  2.1 17.1 %all-to-all-start = ((bf16[8,128,128]{2,1,0:T(8,128)(2,1)}), bf16[8,128,128]{2,1,0:T(8,128)(2,1)S(1)}, u32[]{:S(2)}, u32[]{:S(2)}) async-start(bf16[8,128,128]{2,1,0:T(8,128)(2,1)} %broadcast_in_dim.3), calls=%async_computation | async-start | bytes 524288 | tf_op jit(solution)/shard_map/all_to_all | solution.py:176
  9.8 9.5 %copy-start = (bf16[4,256,256]{2,1,0:T(8,128)(2,1)S(1)}, bf16[4,256,256]{2,1,0:T(8,128)(2,1)}, u32[]{:S(2)}) copy-start(bf16[4,256,256]{2,1,0:T(8,128)(2,1)} %keys.1) | copy-start | bytes 1572868
  9.8 9.5 %copy-start.1 = (bf16[4,256,256]{2,1,0:T(8,128)(2,1)S(1)}, bf16[4,256,256]{2,1,0:T(8,128)(2,1)}, u32[]{:S(2)}) copy-start(bf16[4,256,256]{2,1,0:T(8,128)(2,1)} %values.1) | copy-start | bytes 1572868
  9.8 9.5 %copy-start.3 = (s32[4]{0:T(128)S(1)}, s32[4]{0:T(128)}, u32[]{:S(2)}) copy-start(s32[4]{0:T(128)} %param.10) | copy-start | bytes 52
  9.8 9.5 %collective-permute-start = (bf16[4,256,256]{2,1,0:T(8,128)(2,1)}, bf16[4,256,256]{2,1,0:T(8,128)(2,1)S(1)}, u32[]{:S(2)}, u32[]{:S(2)}) collective-permute-start(bf16[4,256,256]{2,1,0:T(8,128)(2,1)} %keys.1), channel_id=1, source_target_pairs={{0,1},{1,0},{2,3},{3,2},{4,5},{5,4},{6,7},{7,6},{8,9},{9,8},{10,11... | collective-permute-start | bytes 1572872 | tf_op jit(solution)/shard_map/ppermute | solution.py:180
  14.5 4.8 %collective-permute-start.1 = (bf16[4,256,256]{2,1,0:T(8,128)(2,1)}, bf16[4,256,256]{2,1,0:T(8,128)(2,1)S(1)}, u32[]{:S(2)}, u32[]{:S(2)}) collective-permute-start(bf16[4,256,256]{2,1,0:T(8,128)(2,1)} %values.1), channel_id=1, source_target_pairs={{0,1},{1,0},{2,3},{3,2},{4,5},{5,4},{6,7},{7,6},{8,9},{9,8},{10,11... | collective-permute-start | bytes 1572872 | tf_op jit(solution)/shard_map/ppermute | solution.py:181
  21.2 17.2 %all-to-all-start.1 = ((bf16[8,144,128]{2,1,0:T(8,128)(2,1)}), bf16[8,144,128]{2,1,0:T(8,128)(2,1)S(1)}, u32[]{:S(2)}, u32[]{:S(2)}) async-start(bf16[8,144,128]{2,1,0:T(8,128)(2,1)} %attend.1), calls=%async_computation.1 | async-start | bytes 589824 | tf_op jit(solution)/shard_map/all_to_all | solution.py:204
  29.2 26.4 %copy-start.2 = (bf16[128,128]{1,0:T(8,128)(2,1)S(1)}, bf16[128,128]{1,0:T(8,128)(2,1)}, u32[]{:S(2)}) copy-start(bf16[128,128]{1,0:T(8,128)(2,1)} %residual.1) | copy-start | bytes 98308
  55.6 23.0 %copy-start.4 = (f32[128]{0:T(128)S(1)}, f32[128]{0:T(128)}, u32[]{:S(2)}) copy-start(f32[128]{0:T(128)} %param.13) | copy-start | bytes 1540

commit v6 on v4

--- a/solution.py
+++ b/solution.py
@@ -31,6 +31,11 @@
         cost_estimate=pl.CostEstimate(flops=flops, bytes_accessed=moved, transcendentals=0),
         name=name,
     )(*args)
+
+
+def spread_kernel(queries, out):
+    for i in range(out.shape[0]):
+        out[i] = queries[...]
 
 
 def arrange_kernel(queries, out):
@@ -86,9 +91,9 @@
             part = slice(group * HD, (group + 1) * HD)
             staged[2 * request + group, pl.ds(0, HD), :] = (summed[part, part] * inverse[:, part]).astype(BF16)
             staged[2 * request + group, pl.ds(HD, STATS), :] = stats[:, part]
-        pair = pl.ds(2 * request, 2)
-        copies.append(pltpu.make_async_copy(staged.at[pair], out.at[pair], sems.at[request]))
-        copies[-1].start()
+            to = 2 * request + group
+            copies.append(pltpu.make_async_copy(staged.at[to], out.at[to], sems.at[to]))
+            copies[-1].start()
     for copy in copies:
         copy.wait()
 
@@ -153,8 +158,15 @@
     tokens = queries.shape[0]
     depth, groups, width = out_weight.shape
     weight = out_weight.reshape(depth, groups * width)
+    spread = call(
+        spread_kernel,
+        jax.ShapeDtypeStruct((chips, tokens, HD), BF16),
+        (queries,),
+        moved=2**18,
+        name="spread",
+    )
     gathered = lax.all_to_all(
-        jnp.broadcast_to(queries, (chips, tokens, HD)), "y", 0, 0, tiled=True
+        spread, "y", 0, 0, tiled=True
     )
     swap = [(0, 1), (1, 0)]
     other_keys = lax.ppermute(cache_keys, "core", swap)
@@ -175,7 +187,7 @@
         out_specs=pl.BlockSpec(memory_space=pl.ANY),
         scratch=[
             pltpu.VMEM((chips, HD + STATS, HD), BF16),
-            pltpu.SemaphoreType.DMA((cache_keys.shape[0],)),
+            pltpu.SemaphoreType.DMA((chips,)),
         ],
         flops=4 * 2 * 2 * 512 * 256 * HD,
         moved=2**21,

time: 79.3 us -> 79.3 us (level)
    broadcast_in_dim x1 -> x0, local copies, waits for them, and re-layouts: 1.5 us -> none  [on_device(): jnp.broadcast_to(queries, (chips, tokens, HD))]
    pallas_call x6 -> x7, Pallas kernels: 3.45 us -> 4.22 us  [call(): pl.pallas_call(kernel, out_shape=out_shape, in_specs=in_specs or [VMEM] *...]
    unnamed x11 -> x13, local copies, waits for them, and re-layouts: 1.98 us -> 2.73 us
where the time goes in v6:
time: 79.3 us; the launch traced here: 78.7 us
  blocking collectives  38.6 us (49%)
  starting transfers between devices  20.3 us (26%)
  waiting for transfers between devices  12 us (15%)
  Pallas kernels  4.22 us (5%)
  local copies, waits for them, and re-layouts  2.73 us (3%)
    all_to_all x1, blocking collectives, on_device(): lax.all_to_all(squares.reshape(devices, 1, tokens), ('pipe', 'y', 'core')...  14.3 us
    all_to_all x1, blocking collectives, on_device(): half = lax.all_to_all(own, 'y', 0, 0, tiled=True)  11.8 us
    all_to_all x1, waiting for transfers between devices, on_device(): parts = lax.all_to_all(parts, 'y', 0, 0, tiled=True)  9.22 us
    all_to_all x1, starting transfers between devices, on_device(): gathered = lax.all_to_all(spread, 'y', 0, 0, tiled=True)  7.65 us
    all_to_all x1, blocking collectives, on_device(): shares = lax.all_to_all(shares, 'pipe', 0, 0, tiled=True)  7.22 us
    all_to_all x1, starting transfers between devices, on_device(): parts = lax.all_to_all(parts, 'y', 0, 0, tiled=True)  6.06 us
    all_gather x1, blocking collectives, on_device(): attended = lax.all_gather(half, 'core')  5.34 us
    ppermute x1, starting transfers between devices, on_device(): other_keys = lax.ppermute(cache_keys, 'core', swap)  4.69 us
  transfers between devices with their start and end apart: 4, of which 2 were waited for; matrix products, arithmetic and copies ran while one was open for 2% of the time, Pallas kernels for 0%

profile of v6, /device:TPU:1, one launch (start us, length us, event | category | flops | bytes accessed | tf_op | source)
XLA Modules:
  0.0 78.7 jit_solution(1790645653077669076)
XLA Ops:
  0.6 0.7 copy-done.2
  1.4 0.7 spread.1
  2.1 7.7 %all-to-all-start = ((bf16[8,128,128]{2,1,0:T(8,128)(2,1)}), bf16[8,128,128]{2,1,0:T(8,128)(2,1)S(1)}, u32[]{:S(2)}, u32[]{:S(2)}) async-start(bf16[8,128,128]{2,1,0:T(8,128)(2,1)} %spread.1), calls=%async_computation | async-start | bytes 524288 | tf_op jit(solution)/shard_map/all_to_all | solution.py:168
  9.8 0.0 copy-start.1
  9.8 0.0 copy-start.4
  9.8 4.7 %collective-permute-start = (bf16[4,256,256]{2,1,0:T(8,128)(2,1)}, bf16[4,256,256]{2,1,0:T(8,128)(2,1)S(1)}, u32[]{:S(2)}, u32[]{:S(2)}) collective-permute-start(bf16[4,256,256]{2,1,0:T(8,128)(2,1)} %keys.1), channel_id=1, source_target_pairs={{0,1},{1,0},{2,3},{3,2},{4,5},{5,4},{6,7},{7,6},{8,9},{9,8},{10,11... | collective-permute-start | bytes 1572872 | tf_op jit(solution)/shard_map/ppermute | solution.py:172
  14.5 1.9 %collective-permute-start.1 = (bf16[4,256,256]{2,1,0:T(8,128)(2,1)}, bf16[4,256,256]{2,1,0:T(8,128)(2,1)S(1)}, u32[]{:S(2)}, u32[]{:S(2)}) collective-permute-start(bf16[4,256,256]{2,1,0:T(8,128)(2,1)} %values.1), channel_id=1, source_target_pairs={{0,1},{1,0},{2,3},{3,2},{4,5},{5,4},{6,7},{7,6},{8,9},{9,8},{10,11... | collective-permute-start | bytes 1572872 | tf_op jit(solution)/shard_map/ppermute | solution.py:173
  16.4 2.7 %all-to-all-done.queries = bf16[8,128,128]{2,1,0:T(8,128)(2,1)S(1)} async-done(((bf16[8,128,128]{2,1,0:T(8,128)(2,1)}), bf16[8,128,128]{2,1,0:T(8,128)(2,1)S(1)}, u32[]{:S(2)}, u32[]{:S(2)}) %all-to-all-start) | async-done | bytes 262176 | tf_op jit(solution)/shard_map/all_to_all | solution.py:168
  19.2 0.1 arrange.1.queries
  19.3 0.0 collective-permute-done.other_keys
  19.3 0.0 collective-permute-done.1.other_values
  19.3 1.9 %attend.1 = bf16[8,144,128]{2,1,0:T(8,128)(2,1)} custom-call(s32[1,4]{1,0:T(1,128)S(1)} %bitcast.16, bf16[4,256,256]{2,1,0:T(8,128)(2,1)S(1)} %arrange.1.queries, bf16[4,256,256]{2,1,0:T(8,128)(2,1)S(1)} %copy-done, bf16[4,256,256]{2,1,0:T(8,128)(2,1)S(1)} %copy-done.1, bf16[4,256,256]{2,1,0:T(8,128)(2,1)S(1)} %collective-permute-done.other_keys, ...), custom_call_target="tpu_custom_call" | custom-call | flops 268435456 | bytes 2097152 | tf_op jit(solution)/shard_map/attend/pallas_call | solution.py:24
  21.2 6.1 %all-to-all-start.1 = ((bf16[8,144,128]{2,1,0:T(8,128)(2,1)}), bf16[8,144,128]{2,1,0:T(8,128)(2,1)S(1)}, u32[]{:S(2)}, u32[]{:S(2)}) async-start(bf16[8,144,128]{2,1,0:T(8,128)(2,1)} %attend.1), calls=%async_computation.1 | async-start | bytes 589824 | tf_op jit(solution)/shard_map/all_to_all | solution.py:196
  27.3 2.0 %copy.12 = bf16[256,8,4,128]{3,1,2,0:T(8,128)(2,1)S(1)} copy(bf16[256,8,4,128]{3,2,1,0:T(4,128)(2,1)} %bitcast.18) | data formatting | bytes 4194304
  29.2 9.2 %all-to-all-done.1.parts = bf16[8,144,128]{2,1,0:T(8,128)(2,1)S(1)} async-done(((bf16[8,144,128]{2,1,0:T(8,128)(2,1)}), bf16[8,144,128]{2,1,0:T(8,128)(2,1)S(1)}, u32[]{:S(2)}, u32[]{:S(2)}) %all-to-all-start.1) | async-done | bytes 294944 | tf_op jit(solution)/shard_map/all_to_all | solution.py:196
  38.5 0.2 combine.1
  38.6 0.0 copy-start.3
  38.6 11.8 %all_to_all.25 = bf16[8,128,128]{2,1,0:T(8,128)(2,1)S(1)} all-to-all(bf16[8,128,128]{2,1,0:T(8,128)(2,1)S(1)} %combine.1), channel_id=1, replica_groups=mesh['replica'=8,'pipe'=4,'y'=8,'core'=2] {'y'}, dimensions={0} | all-to-all | bytes 524288 | tf_op jit(solution)/shard_map/all_to_all | solution.py:206
  50.5 5.3 %all-gather = bf16[16,128,128]{2,1,0:T(8,128)(2,1)S(1)} all-gather(bf16[8,128,128]{2,1,0:T(8,128)(2,1)S(1)} %all_to_all.25), channel_id=2, replica_groups=mesh['replica'=8,'pipe'=4,'y'=8,'core'=2] {'core'}, dimensions={0}, use_global_device_ids=true | all-gather | bytes 786432 | tf_op jit(solution)/shard_map/all_gather | solution.py:207
  55.8 0.5 project.1
  56.3 7.2 %all_to_all.26.shares = bf16[4,128,128]{2,1,0:T(8,128)(2,1)S(1)} all-to-all(bf16[4,128,128]{2,1,0:T(8,128)(2,1)S(1)} %project.1), channel_id=1, replica_groups=mesh['replica'=8,'pipe'=4,'y'=8,'core'=2] {'pipe'}, dimensions={0} | all-to-all | bytes 262144 | tf_op jit(solution)/shard_map/all_to_all | solution.py:218
  63.5 0.1 update.1
  63.7 14.3 %all_to_all.27 = f32[64,1,128]{2,1,0:T(1,128)S(1)} all-to-all(f32[64,1,128]{2,1,0:T(1,128)S(1)} %bitcast.15), channel_id=1, replica_groups=mesh['replica'=8,'pipe'=4,'y'=8,'core'=2] {'pipe','y','core'}, dimensions={0} | all-to-all | bytes 65536 | tf_op jit(solution)/shard_map/all_to_all | solution.py:230
  77.9 0.7 norm.1
  (8 shorter events, 0.0 us)
Async XLA Ops:
  0.6 0.8 copy-start.2
  2.1 17.1 %all-to-all-start = ((bf16[8,128,128]{2,1,0:T(8,128)(2,1)}), bf16[8,128,128]{2,1,0:T(8,128)(2,1)S(1)}, u32[]{:S(2)}, u32[]{:S(2)}) async-start(bf16[8,128,128]{2,1,0:T(8,128)(2,1)} %spread.1), calls=%async_computation | async-start | bytes 524288 | tf_op jit(solution)/shard_map/all_to_all | solution.py:168
  9.8 9.5 %copy-start = (bf16[4,256,256]{2,1,0:T(8,128)(2,1)S(1)}, bf16[4,256,256]{2,1,0:T(8,128)(2,1)}, u32[]{:S(2)}) copy-start(bf16[4,256,256]{2,1,0:T(8,128)(2,1)} %keys.1) | copy-start | bytes 1572868
  9.8 9.5 %copy-start.1 = (bf16[4,256,256]{2,1,0:T(8,128)(2,1)S(1)}, bf16[4,256,256]{2,1,0:T(8,128)(2,1)}, u32[]{:S(2)}) copy-start(bf16[4,256,256]{2,1,0:T(8,128)(2,1)} %values.1) | copy-start | bytes 1572868
  9.8 9.5 %copy-start.4 = (s32[4]{0:T(128)S(1)}, s32[4]{0:T(128)}, u32[]{:S(2)}) copy-start(s32[4]{0:T(128)} %param.10) | copy-start | bytes 52
  9.8 9.5 %collective-permute-start = (bf16[4,256,256]{2,1,0:T(8,128)(2,1)}, bf16[4,256,256]{2,1,0:T(8,128)(2,1)S(1)}, u32[]{:S(2)}, u32[]{:S(2)}) collective-permute-start(bf16[4,256,256]{2,1,0:T(8,128)(2,1)} %keys.1), channel_id=1, source_target_pairs={{0,1},{1,0},{2,3},{3,2},{4,5},{5,4},{6,7},{7,6},{8,9},{9,8},{10,11... | collective-permute-start | bytes 1572872 | tf_op jit(solution)/shard_map/ppermute | solution.py:172
  14.5 4.8 %collective-permute-start.1 = (bf16[4,256,256]{2,1,0:T(8,128)(2,1)}, bf16[4,256,256]{2,1,0:T(8,128)(2,1)S(1)}, u32[]{:S(2)}, u32[]{:S(2)}) collective-permute-start(bf16[4,256,256]{2,1,0:T(8,128)(2,1)} %values.1), channel_id=1, source_target_pairs={{0,1},{1,0},{2,3},{3,2},{4,5},{5,4},{6,7},{7,6},{8,9},{9,8},{10,11... | collective-permute-start | bytes 1572872 | tf_op jit(solution)/shard_map/ppermute | solution.py:173
  21.2 17.2 %all-to-all-start.1 = ((bf16[8,144,128]{2,1,0:T(8,128)(2,1)}), bf16[8,144,128]{2,1,0:T(8,128)(2,1)S(1)}, u32[]{:S(2)}, u32[]{:S(2)}) async-start(bf16[8,144,128]{2,1,0:T(8,128)(2,1)} %attend.1), calls=%async_computation.1 | async-start | bytes 589824 | tf_op jit(solution)/shard_map/all_to_all | solution.py:196
  38.6 24.9 %copy-start.3 = (bf16[128,128]{1,0:T(8,128)(2,1)S(1)}, bf16[128,128]{1,0:T(8,128)(2,1)}, u32[]{:S(2)}) copy-start(bf16[128,128]{1,0:T(8,128)(2,1)} %residual.1) | copy-start | bytes 98308
  50.5 27.4 %copy-start.5 = (f32[128]{0:T(128)S(1)}, f32[128]{0:T(128)}, u32[]{:S(2)}) copy-start(f32[128]{0:T(128)} %param.13) | copy-start | bytes 1540

commit v7 on v3

--- a/solution.py
+++ b/solution.py
@@ -87,8 +87,7 @@
             out[2 * request + group, pl.ds(HD, STATS), :] = stats[:, part]
 
 
-def combine_kernel(parts, weight, out):
-    del weight
+def combine_kernel(parts, out):
     count = parts.shape[0]
     stats = [parts[i, pl.ds(HD, STATS), :].astype(F32) for i in range(count)]
     peaks = [s[0:1] for s in stats]
@@ -175,8 +174,7 @@
     own = call(
         combine_kernel,
         jax.ShapeDtypeStruct((chips, HD, HD), BF16),
-        (parts, weight),
-        in_specs=[VMEM, pl.BlockSpec(memory_space=pl.ANY)],
+        (parts,),
         flops=2 * 8 * HD * HD,
         moved=2**19,
         name="combine",

time: 79.3 us -> 81.4 us (1.026)
  blocking collectives: 38.6 us -> 43.8 us
  starting transfers between devices: 20.3 us -> 17.7 us
    all_to_all x1, blocking collectives: 11.8 us -> 18.7 us  [on_device(): parts = lax.all_to_all(parts, 'y', 0, 0, tiled=True)]
    all_to_all x1, starting transfers between devices: 6.05 us -> 3.41 us  [on_device(): half = lax.all_to_all(own, 'y', 0, 0, tiled=True)]
    all_gather x1, blocking collectives: 5.34 us -> 3.81 us  [on_device(): attended = lax.all_gather(half, 'core')]
where the time goes in v7:
time: 81.4 us; the launch traced here: 80.8 us
  blocking collectives  43.8 us (54%)
  starting transfers between devices  17.7 us (22%)
  waiting for transfers between devices  11.5 us (14%)
  Pallas kernels  3.56 us (4%)
  local copies, waits for them, and re-layouts  3.48 us (4%)
    all_to_all x1, blocking collectives, on_device(): parts = lax.all_to_all(parts, 'y', 0, 0, tiled=True)  18.7 us
    all_to_all x1, blocking collectives, on_device(): lax.all_to_all(squares.reshape(devices, 1, tokens), ('pipe', 'y', 'core')...  14.1 us
    all_to_all x1, waiting for transfers between devices, on_device(): half = lax.all_to_all(own, 'y', 0, 0, tiled=True)  8.74 us
    all_to_all x1, starting transfers between devices, on_device(): lax.all_to_all(jnp.broadcast_to(queries, (chips, tokens, HD)), 'y', 0, 0,...  7.65 us
    all_to_all x1, blocking collectives, on_device(): shares = lax.all_to_all(shares, 'pipe', 0, 0, tiled=True)  7.23 us
    ppermute x1, starting transfers between devices, on_device(): other_keys = lax.ppermute(cache_keys, 'core', swap)  4.69 us
    all_gather x1, blocking collectives, on_device(): attended = lax.all_gather(half, 'core')  3.81 us
    pallas_call x6, Pallas kernels, call(): pl.pallas_call(kernel, out_shape=out_shape, in_specs=in_specs or [VMEM] *...  3.56 us
  transfers between devices with their start and end apart: 4, of which 2 were waited for; matrix products, arithmetic and copies ran while one was open for 2% of the time, Pallas kernels for 0%

profile of v7, /device:TPU:1, one launch (start us, length us, event | category | flops | bytes accessed | tf_op | source)
XLA Modules:
  0.0 80.8 jit_solution(15377059598540115578)
XLA Ops:
  0.6 1.5 %broadcast_in_dim.3 = bf16[8,128,128]{2,1,0:T(8,128)(2,1)} broadcast(bf16[128,128]{1,0:T(8,128)(2,1)} %param.7), dimensions={1,2} | broadcast | bytes 294912 | tf_op jit(solution)/shard_map/broadcast_in_dim | solution.py:150
  2.1 7.7 %all-to-all-start = ((bf16[8,128,128]{2,1,0:T(8,128)(2,1)}), bf16[8,128,128]{2,1,0:T(8,128)(2,1)S(1)}, u32[]{:S(2)}, u32[]{:S(2)}) async-start(bf16[8,128,128]{2,1,0:T(8,128)(2,1)} %broadcast_in_dim.3), calls=%async_computation | async-start | bytes 524288 | tf_op jit(solution)/shard_map/all_to_all | solution.py:149
  9.8 0.0 copy-start.1
  9.8 0.0 copy-start.3
  9.8 4.7 %collective-permute-start = (bf16[4,256,256]{2,1,0:T(8,128)(2,1)}, bf16[4,256,256]{2,1,0:T(8,128)(2,1)S(1)}, u32[]{:S(2)}, u32[]{:S(2)}) collective-permute-start(bf16[4,256,256]{2,1,0:T(8,128)(2,1)} %keys.1), channel_id=1, source_target_pairs={{0,1},{1,0},{2,3},{3,2},{4,5},{5,4},{6,7},{7,6},{8,9},{9,8},{10,11... | collective-permute-start | bytes 1572872 | tf_op jit(solution)/shard_map/ppermute | solution.py:153
  14.5 1.9 %collective-permute-start.1 = (bf16[4,256,256]{2,1,0:T(8,128)(2,1)}, bf16[4,256,256]{2,1,0:T(8,128)(2,1)S(1)}, u32[]{:S(2)}, u32[]{:S(2)}) collective-permute-start(bf16[4,256,256]{2,1,0:T(8,128)(2,1)} %values.1), channel_id=1, source_target_pairs={{0,1},{1,0},{2,3},{3,2},{4,5},{5,4},{6,7},{7,6},{8,9},{9,8},{10,11... | collective-permute-start | bytes 1572872 | tf_op jit(solution)/shard_map/ppermute | solution.py:154
  16.4 2.7 %all-to-all-done.queries = bf16[8,128,128]{2,1,0:T(8,128)(2,1)S(1)} async-done(((bf16[8,128,128]{2,1,0:T(8,128)(2,1)}), bf16[8,128,128]{2,1,0:T(8,128)(2,1)S(1)}, u32[]{:S(2)}, u32[]{:S(2)}) %all-to-all-start) | async-done | bytes 262176 | tf_op jit(solution)/shard_map/all_to_all | solution.py:149
  19.2 0.1 arrange.1.queries
  19.3 0.0 collective-permute-done.other_keys
  19.3 0.0 collective-permute-done.1.other_values
  19.3 1.2 %attend.1 = bf16[8,144,128]{2,1,0:T(8,128)(2,1)S(1)} custom-call(s32[1,4]{1,0:T(1,128)S(1)} %bitcast.15, bf16[4,256,256]{2,1,0:T(8,128)(2,1)S(1)} %arrange.1.queries, bf16[4,256,256]{2,1,0:T(8,128)(2,1)S(1)} %copy-done, bf16[4,256,256]{2,1,0:T(8,128)(2,1)S(1)} %copy-done.1, bf16[4,256,256]{2,1,0:T(8,128)(2,1)S(1)} %collective-permute-done.other_keys, ...), custom_call_target="tpu_custom_call" | custom-call | flops 268435456 | bytes 2097152 | tf_op jit(solution)/shard_map/attend/pallas_call | solution.py:24
  20.6 18.7 %all_to_all.25.parts = bf16[8,144,128]{2,1,0:T(8,128)(2,1)S(1)} all-to-all(bf16[8,144,128]{2,1,0:T(8,128)(2,1)S(1)} %attend.1), channel_id=1, replica_groups=mesh['replica'=8,'pipe'=4,'y'=8,'core'=2] {'y'}, dimensions={0} | all-to-all | bytes 589824 | tf_op jit(solution)/shard_map/all_to_all | solution.py:173
  39.2 0.9 %combine.1 = bf16[8,128,128]{2,1,0:T(8,128)(2,1)} custom-call(bf16[8,144,128]{2,1,0:T(8,128)(2,1)S(1)} %all_to_all.25.parts), custom_call_target="tpu_custom_call" | custom-call | flops 262144 | bytes 524288 | tf_op jit(solution)/shard_map/combine/pallas_call | solution.py:24
  40.1 3.4 %all-to-all-start.2 = ((bf16[8,128,128]{2,1,0:T(8,128)(2,1)}), bf16[8,128,128]{2,1,0:T(8,128)(2,1)S(1)}, u32[]{:S(2)}, u32[]{:S(2)}) async-start(bf16[8,128,128]{2,1,0:T(8,128)(2,1)} %combine.1), calls=%async_computation.2 | async-start | bytes 524288 | tf_op jit(solution)/shard_map/all_to_all | solution.py:182
  43.5 2.0 %copy.12 = bf16[256,8,4,128]{3,1,2,0:T(8,128)(2,1)S(1)} copy(bf16[256,8,4,128]{3,2,1,0:T(4,128)(2,1)} %bitcast.17) | data formatting | bytes 4194304
  45.5 0.0 copy-start.2
  45.5 0.0 copy-start.4
  45.5 8.7 %all-to-all-done.2 = bf16[8,128,128]{2,1,0:T(8,128)(2,1)S(1)} async-done(((bf16[8,128,128]{2,1,0:T(8,128)(2,1)}), bf16[8,128,128]{2,1,0:T(8,128)(2,1)S(1)}, u32[]{:S(2)}, u32[]{:S(2)}) %all-to-all-start.2) | async-done | bytes 262176 | tf_op jit(solution)/shard_map/all_to_all | solution.py:182
  54.2 3.8 %all-gather = bf16[16,128,128]{2,1,0:T(8,128)(2,1)S(1)} all-gather(bf16[8,128,128]{2,1,0:T(8,128)(2,1)S(1)} %all-to-all-done.2), channel_id=2, replica_groups=mesh['replica'=8,'pipe'=4,'y'=8,'core'=2] {'core'}, dimensions={0}, use_global_device_ids=true | all-gather | bytes 786432 | tf_op jit(solution)/shard_map/all_gather | solution.py:183
  58.0 0.5 project.1
  58.6 7.2 %all_to_all.26.shares = bf16[4,128,128]{2,1,0:T(8,128)(2,1)S(1)} all-to-all(bf16[4,128,128]{2,1,0:T(8,128)(2,1)S(1)} %project.1), channel_id=1, replica_groups=mesh['replica'=8,'pipe'=4,'y'=8,'core'=2] {'pipe'}, dimensions={0} | all-to-all | bytes 262144 | tf_op jit(solution)/shard_map/all_to_all | solution.py:194
  65.8 0.1 update.1
  65.9 14.1 %all_to_all.27 = f32[64,1,128]{2,1,0:T(1,128)S(1)} all-to-all(f32[64,1,128]{2,1,0:T(1,128)S(1)} %bitcast.14), channel_id=1, replica_groups=mesh['replica'=8,'pipe'=4,'y'=8,'core'=2] {'pipe','y','core'}, dimensions={0} | all-to-all | bytes 65536 | tf_op jit(solution)/shard_map/all_to_all | solution.py:206
  80.1 0.7 norm.1
  (6 shorter events, 0.0 us)
Async XLA Ops:
  2.1 17.1 %all-to-all-start = ((bf16[8,128,128]{2,1,0:T(8,128)(2,1)}), bf16[8,128,128]{2,1,0:T(8,128)(2,1)S(1)}, u32[]{:S(2)}, u32[]{:S(2)}) async-start(bf16[8,128,128]{2,1,0:T(8,128)(2,1)} %broadcast_in_dim.3), calls=%async_computation | async-start | bytes 524288 | tf_op jit(solution)/shard_map/all_to_all | solution.py:149
  9.8 9.5 %copy-start = (bf16[4,256,256]{2,1,0:T(8,128)(2,1)S(1)}, bf16[4,256,256]{2,1,0:T(8,128)(2,1)}, u32[]{:S(2)}) copy-start(bf16[4,256,256]{2,1,0:T(8,128)(2,1)} %keys.1) | copy-start | bytes 1572868
  9.8 9.5 %copy-start.1 = (bf16[4,256,256]{2,1,0:T(8,128)(2,1)S(1)}, bf16[4,256,256]{2,1,0:T(8,128)(2,1)}, u32[]{:S(2)}) copy-start(bf16[4,256,256]{2,1,0:T(8,128)(2,1)} %values.1) | copy-start | bytes 1572868
  9.8 9.5 %copy-start.3 = (s32[4]{0:T(128)S(1)}, s32[4]{0:T(128)}, u32[]{:S(2)}) copy-start(s32[4]{0:T(128)} %param.10) | copy-start | bytes 52
  9.8 9.5 %collective-permute-start = (bf16[4,256,256]{2,1,0:T(8,128)(2,1)}, bf16[4,256,256]{2,1,0:T(8,128)(2,1)S(1)}, u32[]{:S(2)}, u32[]{:S(2)}) collective-permute-start(bf16[4,256,256]{2,1,0:T(8,128)(2,1)} %keys.1), channel_id=1, source_target_pairs={{0,1},{1,0},{2,3},{3,2},{4,5},{5,4},{6,7},{7,6},{8,9},{9,8},{10,11... | collective-permute-start | bytes 1572872 | tf_op jit(solution)/shard_map/ppermute | solution.py:153
  14.5 4.8 %collective-permute-start.1 = (bf16[4,256,256]{2,1,0:T(8,128)(2,1)}, bf16[4,256,256]{2,1,0:T(8,128)(2,1)S(1)}, u32[]{:S(2)}, u32[]{:S(2)}) collective-permute-start(bf16[4,256,256]{2,1,0:T(8,128)(2,1)} %values.1), channel_id=1, source_target_pairs={{0,1},{1,0},{2,3},{3,2},{4,5},{5,4},{6,7},{7,6},{8,9},{9,8},{10,11... | collective-permute-start | bytes 1572872 | tf_op jit(solution)/shard_map/ppermute | solution.py:154
  40.1 14.1 %all-to-all-start.2 = ((bf16[8,128,128]{2,1,0:T(8,128)(2,1)}), bf16[8,128,128]{2,1,0:T(8,128)(2,1)S(1)}, u32[]{:S(2)}, u32[]{:S(2)}) async-start(bf16[8,128,128]{2,1,0:T(8,128)(2,1)} %combine.1), calls=%async_computation.2 | async-start | bytes 524288 | tf_op jit(solution)/shard_map/all_to_all | solution.py:182
  45.5 20.3 %copy-start.2 = (bf16[128,128]{1,0:T(8,128)(2,1)S(1)}, bf16[128,128]{1,0:T(8,128)(2,1)}, u32[]{:S(2)}) copy-start(bf16[128,128]{1,0:T(8,128)(2,1)} %residual.1) | copy-start | bytes 98308
  45.5 34.6 %copy-start.4 = (f32[128]{0:T(128)S(1)}, f32[128]{0:T(128)}, u32[]{:S(2)}) copy-start(f32[128]{0:T(128)} %param.13) | copy-start | bytes 1540

commit v8 on v7

--- a/solution.py
+++ b/solution.py
@@ -33,7 +33,8 @@
     )(*args)
 
 
-def arrange_kernel(queries, out):
+def arrange_kernel(queries, weight, out):
+    del weight
     heads = queries.shape[0] // 2
     rows = heads * SPAN
     blank = jnp.zeros((rows, HD), BF16)
@@ -47,7 +48,7 @@
                 )
 
 
-def attend_kernel(prefix, queries, keys, values, other_keys, other_values, out):
+def attend_kernel(prefix, queries, keys, values, far_keys, far_values, out, other_keys, other_values, sems):
     requests, slots, width = keys.shape
     rows = width
     slot = lax.broadcasted_iota(jnp.int32, (slots, rows), 0)
@@ -57,7 +58,19 @@
     chunk = 2 * lax.axis_index("y") + core
     offsets = (lane - chunk * slots, lane - (chunk + 1 - 2 * core) * slots)
     scale = math.log2(math.e) / math.sqrt(HD)
+    loads = [
+        [
+            pltpu.make_async_copy(source.at[r], target.at[r], sems.at[i, r])
+            for i, (source, target) in enumerate(((far_keys, other_keys), (far_values, other_values)))
+        ]
+        for r in range(requests)
+    ]
+    for pair in loads:
+        for load in pair:
+            load.start()
     for request in range(requests):
+        for load in loads[request]:
+            load.wait()
         wanted = queries[request]
         scores = []
         for key, offset in zip((keys, other_keys), offsets):
@@ -156,7 +169,8 @@
     arranged = call(
         arrange_kernel,
         jax.ShapeDtypeStruct((cache_keys.shape[0], 2 * HD, 2 * HD), BF16),
-        (gathered,),
+        (gathered, weight),
+        in_specs=[VMEM, pl.BlockSpec(memory_space=pl.ANY)],
         flops=2**30,
         moved=2**19,
         name="arrange",
@@ -165,7 +179,12 @@
         attend_kernel,
         jax.ShapeDtypeStruct((chips, HD + STATS, HD), BF16),
         (prefix_lengths.reshape(1, -1), arranged, cache_keys, cache_values, other_keys, other_values),
-        in_specs=[VMEM] * 6,
+        in_specs=[VMEM] * 4 + [pl.BlockSpec(memory_space=pltpu.HBM)] * 2,
+        scratch=[
+            pltpu.VMEM(cache_keys.shape, BF16),
+            pltpu.VMEM(cache_values.shape, BF16),
+            pltpu.SemaphoreType.DMA((2, cache_keys.shape[0])),
+        ],
         flops=4 * 2 * 2 * 512 * 256 * HD,
         moved=2**21,
         name="attend",

time: 81.4 us -> 82.1 us (level)
  blocking collectives: 43.8 us -> 56.7 us
  waiting for transfers between devices: 11.5 us -> 0.92 us
  starting transfers between devices: 17.7 us -> 14.1 us
  Pallas kernels: 3.56 us -> 5.32 us
    all_to_all x0 -> x1, blocking collectives: none -> 11.6 us  [on_device(): half = lax.all_to_all(own, 'y', 0, 0, tiled=True)]
    all_to_all x1 -> x0, waiting for transfers between devices: 8.74 us -> none  [on_device(): half = lax.all_to_all(own, 'y', 0, 0, tiled=True)]
    all_to_all x1 -> x0, starting transfers between devices: 3.41 us -> none  [on_device(): half = lax.all_to_all(own, 'y', 0, 0, tiled=True)]
    all_to_all x1, waiting for transfers between devices: 2.75 us -> 0.92 us  [on_device(): lax.all_to_all(jnp.broadcast_to(queries, (chips, tokens, HD)), 'y', 0, 0,...]
    all_gather x1, blocking collectives: 3.81 us -> 5.59 us  [on_device(): attended = lax.all_gather(half, 'core')]
    pallas_call x6, Pallas kernels: 3.56 us -> 5.32 us  [call(): pl.pallas_call(kernel, out_shape=out_shape, in_specs=in_specs or [VMEM] *...]
  transfers between devices with their start and end apart: 4 -> 3, of which waited for: 2 -> 1; matrix products, arithmetic and copies ran while one was open for 2% -> 2% of each run, Pallas kernels for 0% -> 0%
where the time goes in v8:
time: 82.1 us; the launch traced here: 81.5 us
  blocking collectives  56.7 us (69%)
  starting transfers between devices  14.1 us (17%)
  Pallas kernels  5.32 us (6%)
  local copies, waits for them, and re-layouts  3.63 us (4%)
  waiting for transfers between devices  0.92 us (1%)
    all_to_all x1, blocking collectives, on_device(): parts = lax.all_to_all(parts, 'y', 0, 0, tiled=True)  18.1 us
    all_to_all x1, blocking collectives, on_device(): lax.all_to_all(squares.reshape(devices, 1, tokens), ('pipe', 'y', 'core')...  14.2 us
    all_to_all x1, blocking collectives, on_device(): half = lax.all_to_all(own, 'y', 0, 0, tiled=True)  11.6 us
    all_to_all x1, starting transfers between devices, on_device(): lax.all_to_all(jnp.broadcast_to(queries, (chips, tokens, HD)), 'y', 0, 0,...  7.65 us
    all_to_all x1, blocking collectives, on_device(): shares = lax.all_to_all(shares, 'pipe', 0, 0, tiled=True)  7.22 us
    all_gather x1, blocking collectives, on_device(): attended = lax.all_gather(half, 'core')  5.59 us
    pallas_call x6, Pallas kernels, call(): pl.pallas_call(kernel, out_shape=out_shape, in_specs=in_specs or [VMEM] *...  5.32 us
    ppermute x1, starting transfers between devices, on_device(): other_keys = lax.ppermute(cache_keys, 'core', swap)  4.56 us
  transfers between devices with their start and end apart: 3, of which 1 were waited for; matrix products, arithmetic and copies ran while one was open for 2% of the time, Pallas kernels for 0%

profile of v8, /device:TPU:1, one launch (start us, length us, event | category | flops | bytes accessed | tf_op | source)
XLA Modules:
  0.0 81.5 jit_solution(5244144406535508910)
XLA Ops:
  0.6 1.5 %broadcast_in_dim.3 = bf16[8,128,128]{2,1,0:T(8,128)(2,1)} broadcast(bf16[128,128]{1,0:T(8,128)(2,1)} %param.7), dimensions={1,2} | broadcast | bytes 294912 | tf_op jit(solution)/shard_map/broadcast_in_dim | solution.py:163
  2.1 7.7 %all-to-all-start = ((bf16[8,128,128]{2,1,0:T(8,128)(2,1)}), bf16[8,128,128]{2,1,0:T(8,128)(2,1)S(1)}, u32[]{:S(2)}, u32[]{:S(2)}) async-start(bf16[8,128,128]{2,1,0:T(8,128)(2,1)} %broadcast_in_dim.3), calls=%async_computation | async-start | bytes 524288 | tf_op jit(solution)/shard_map/all_to_all | solution.py:162
  9.8 4.6 %collective-permute-start = (bf16[4,256,256]{2,1,0:T(8,128)(2,1)}, bf16[4,256,256]{2,1,0:T(8,128)(2,1)}, u32[]{:S(2)}, u32[]{:S(2)}) collective-permute-start(bf16[4,256,256]{2,1,0:T(8,128)(2,1)} %keys.1), channel_id=1, source_target_pairs={{0,1},{1,0},{2,3},{3,2},{4,5},{5,4},{6,7},{7,6},{8,9},{9,8},{10,11... | collective-permute-start | bytes 1572872 | tf_op jit(solution)/shard_map/ppermute | solution.py:166
  14.3 1.9 %collective-permute-start.1 = (bf16[4,256,256]{2,1,0:T(8,128)(2,1)}, bf16[4,256,256]{2,1,0:T(8,128)(2,1)}, u32[]{:S(2)}, u32[]{:S(2)}) collective-permute-start(bf16[4,256,256]{2,1,0:T(8,128)(2,1)} %values.1), channel_id=1, source_target_pairs={{0,1},{1,0},{2,3},{3,2},{4,5},{5,4},{6,7},{7,6},{8,9},{9,8},{10,11... | collective-permute-start | bytes 1572872 | tf_op jit(solution)/shard_map/ppermute | solution.py:167
  16.3 2.0 %copy.12 = bf16[256,8,4,128]{3,1,2,0:T(8,128)(2,1)S(1)} copy(bf16[256,8,4,128]{3,2,1,0:T(4,128)(2,1)} %bitcast.18) | data formatting | bytes 4194304
  18.2 0.0 copy-start
  18.2 0.0 copy-start.1
  18.3 0.0 copy-start.3
  18.3 0.9 %all-to-all-done.queries = bf16[8,128,128]{2,1,0:T(8,128)(2,1)S(1)} async-done(((bf16[8,128,128]{2,1,0:T(8,128)(2,1)}), bf16[8,128,128]{2,1,0:T(8,128)(2,1)S(1)}, u32[]{:S(2)}, u32[]{:S(2)}) %all-to-all-start) | async-done | bytes 262176 | tf_op jit(solution)/shard_map/all_to_all | solution.py:162
  19.2 0.1 arrange.1.queries
  19.3 0.0 collective-permute-done.far_keys
  19.3 0.0 collective-permute-done.1.far_values
  19.3 0.1 copy-done.1
  19.4 3.7 %attend.1 = bf16[8,144,128]{2,1,0:T(8,128)(2,1)S(1)} custom-call(s32[1,4]{1,0:T(1,128)S(1)} %bitcast.16, bf16[4,256,256]{2,1,0:T(8,128)(2,1)S(1)} %arrange.1.queries, bf16[4,256,256]{2,1,0:T(8,128)(2,1)S(1)} %copy-done, bf16[4,256,256]{2,1,0:T(8,128)(2,1)S(1)} %copy-done.1, bf16[4,256,256]{2,1,0:T(8,128)(2,1)} %collective-permute-done.far_keys, ...), custom_call_target="tpu_custom_call" | custom-call | flops 268435456 | bytes 2097152 | tf_op jit(solution)/shard_map/attend/pallas_call | solution.py:24
  23.2 18.1 %all_to_all.25.parts = bf16[8,144,128]{2,1,0:T(8,128)(2,1)S(1)} all-to-all(bf16[8,144,128]{2,1,0:T(8,128)(2,1)S(1)} %attend.1), channel_id=1, replica_groups=mesh['replica'=8,'pipe'=4,'y'=8,'core'=2] {'y'}, dimensions={0} | all-to-all | bytes 589824 | tf_op jit(solution)/shard_map/all_to_all | solution.py:192
  41.3 0.2 combine.1
  41.5 0.0 copy-start.2
  41.5 11.6 %all_to_all.26 = bf16[8,128,128]{2,1,0:T(8,128)(2,1)S(1)} all-to-all(bf16[8,128,128]{2,1,0:T(8,128)(2,1)S(1)} %combine.1), channel_id=1, replica_groups=mesh['replica'=8,'pipe'=4,'y'=8,'core'=2] {'y'}, dimensions={0} | all-to-all | bytes 524288 | tf_op jit(solution)/shard_map/all_to_all | solution.py:201
  53.1 5.6 %all-gather = bf16[16,128,128]{2,1,0:T(8,128)(2,1)S(1)} all-gather(bf16[8,128,128]{2,1,0:T(8,128)(2,1)S(1)} %all_to_all.26), channel_id=2, replica_groups=mesh['replica'=8,'pipe'=4,'y'=8,'core'=2] {'core'}, dimensions={0}, use_global_device_ids=true | all-gather | bytes 786432 | tf_op jit(solution)/shard_map/all_gather | solution.py:202
  58.7 0.5 project.1
  59.2 7.2 %all_to_all.27.shares = bf16[4,128,128]{2,1,0:T(8,128)(2,1)S(1)} all-to-all(bf16[4,128,128]{2,1,0:T(8,128)(2,1)S(1)} %project.1), channel_id=1, replica_groups=mesh['replica'=8,'pipe'=4,'y'=8,'core'=2] {'pipe'}, dimensions={0} | all-to-all | bytes 262144 | tf_op jit(solution)/shard_map/all_to_all | solution.py:213
  66.4 0.1 update.1
  66.5 14.2 %all_to_all.28 = f32[64,1,128]{2,1,0:T(1,128)S(1)} all-to-all(f32[64,1,128]{2,1,0:T(1,128)S(1)} %bitcast.15), channel_id=1, replica_groups=mesh['replica'=8,'pipe'=4,'y'=8,'core'=2] {'pipe','y','core'}, dimensions={0} | all-to-all | bytes 65536 | tf_op jit(solution)/shard_map/all_to_all | solution.py:225
  80.7 0.7 norm.1
  (5 shorter events, 0.0 us)
Async XLA Ops:
  2.1 17.1 %all-to-all-start = ((bf16[8,128,128]{2,1,0:T(8,128)(2,1)}), bf16[8,128,128]{2,1,0:T(8,128)(2,1)S(1)}, u32[]{:S(2)}, u32[]{:S(2)}) async-start(bf16[8,128,128]{2,1,0:T(8,128)(2,1)} %broadcast_in_dim.3), calls=%async_computation | async-start | bytes 524288 | tf_op jit(solution)/shard_map/all_to_all | solution.py:162
  9.8 9.5 %collective-permute-start = (bf16[4,256,256]{2,1,0:T(8,128)(2,1)}, bf16[4,256,256]{2,1,0:T(8,128)(2,1)}, u32[]{:S(2)}, u32[]{:S(2)}) collective-permute-start(bf16[4,256,256]{2,1,0:T(8,128)(2,1)} %keys.1), channel_id=1, source_target_pairs={{0,1},{1,0},{2,3},{3,2},{4,5},{5,4},{6,7},{7,6},{8,9},{9,8},{10,11... | collective-permute-start | bytes 1572872 | tf_op jit(solution)/shard_map/ppermute | solution.py:166
  14.3 4.9 %collective-permute-start.1 = (bf16[4,256,256]{2,1,0:T(8,128)(2,1)}, bf16[4,256,256]{2,1,0:T(8,128)(2,1)}, u32[]{:S(2)}, u32[]{:S(2)}) collective-permute-start(bf16[4,256,256]{2,1,0:T(8,128)(2,1)} %values.1), channel_id=1, source_target_pairs={{0,1},{1,0},{2,3},{3,2},{4,5},{5,4},{6,7},{7,6},{8,9},{9,8},{10,11... | collective-permute-start | bytes 1572872 | tf_op jit(solution)/shard_map/ppermute | solution.py:167
  18.2 1.1 %copy-start = (bf16[4,256,256]{2,1,0:T(8,128)(2,1)S(1)}, bf16[4,256,256]{2,1,0:T(8,128)(2,1)}, u32[]{:S(2)}) copy-start(bf16[4,256,256]{2,1,0:T(8,128)(2,1)} %keys.1) | copy-start | bytes 1572868
  18.2 1.2 %copy-start.1 = (bf16[4,256,256]{2,1,0:T(8,128)(2,1)S(1)}, bf16[4,256,256]{2,1,0:T(8,128)(2,1)}, u32[]{:S(2)}) copy-start(bf16[4,256,256]{2,1,0:T(8,128)(2,1)} %values.1) | copy-start | bytes 1572868
  18.3 1.2 %copy-start.3 = (s32[4]{0:T(128)S(1)}, s32[4]{0:T(128)}, u32[]{:S(2)}) copy-start(s32[4]{0:T(128)} %param.10) | copy-start | bytes 52
  41.5 24.9 %copy-start.2 = (bf16[128,128]{1,0:T(8,128)(2,1)S(1)}, bf16[128,128]{1,0:T(8,128)(2,1)}, u32[]{:S(2)}) copy-start(bf16[128,128]{1,0:T(8,128)(2,1)} %residual.1) | copy-start | bytes 98308
  53.1 27.6 %copy-start.4 = (f32[128]{0:T(128)S(1)}, f32[128]{0:T(128)}, u32[]{:S(2)}) copy-start(f32[128]{0:T(128)} %param.13) | copy-start | bytes 1540
